TPU v7x, 32 devices: a whole 2x2x4 slice. The times are simulated.
32 devices in a mesh: gx: 8 (over y, x, core), gy: 4 (over z).
Axes of the slice: x: 2, y: 2, z: 4, core: 2. Of those that a mesh axis runs over, the one named last changes fastest.
Arguments:
- density: float32 [256, 256, 128], P('gx', 'gy'), may hold values from 0 to 1
- transfer_table: int32 [4, 128], replicated, may hold values from 0 to 255
- shear_x: int32 [2, 256], P(None, 'gx'), may hold values from -16 to 15, as said below
- shear_y: int32 [2, 256], P(None, 'gy'), may hold values from -16 to 15, as said below
- direction: int32 [2, 2], replicated, may hold values from 0 to 1
Outputs:
- image_x: float32 [2, 4, 256, 128], P(None, None, ('gy', 'gx'))
- image_y: float32 [2, 4, 256, 128], P(None, None, ('gx', 'gy'))
Inputs may be any that keep to these rules, and one draw needn't show every extreme that they name: `shear_x`: the shift along z of a slice in a view. `shear_y`: the shift along z of a slice in a view.
All inputs are finite; a program needn't handle non-finite values.
Results may differ from a plain program's by a relative error of at most 0.0003.
Values sent between devices are 32-bit elements; how exact they have to be, the bound alone decides.
A program may use at most 192 MiB of HBM per device.

v0:
```python
import math

import jax
import jax.numpy as jnp
from jax import lax
from jax.sharding import PartitionSpec as P

SHEAR = 16


light_x = 1.0 / 3.0
light_y = 2.0 / 3.0
light_z = 2.0 / 3.0
highest = lax.Precision.HIGHEST


def with_halo(block, sides, width):
    for axis, dim in sides:
        count = lax.axis_size(axis)
        forward = [(i, i + 1) for i in range(count - 1)]
        backward = [(target, source) for source, target in forward]
        low = lax.ppermute(
            lax.slice_in_dim(block, block.shape[dim] - width, None, axis=dim), axis, forward
        )
        high = lax.ppermute(lax.slice_in_dim(block, 0, width, axis=dim), axis, backward)
        block = jnp.concatenate([low, block, high], axis=dim)
    return block


def shading(padded):
    framed = jnp.pad(padded, ((0, 0), (0, 0), (1, 1)))
    grad_x = (framed[2:, 1:-1, 1:-1] - framed[:-2, 1:-1, 1:-1]) * 0.5
    grad_y = (framed[1:-1, 2:, 1:-1] - framed[1:-1, :-2, 1:-1]) * 0.5
    grad_z = (framed[1:-1, 1:-1, 2:] - framed[1:-1, 1:-1, :-2]) * 0.5
    facing = jnp.abs(light_x * grad_x + light_y * grad_y + light_z * grad_z)
    return 0.3 + 0.7 * facing / jnp.sqrt(grad_x * grad_x + grad_y * grad_y + grad_z * grad_z + 0.01)


def lookup(values, transfer_table):
    knot_count = transfer_table.shape[1]
    levels = transfer_table.astype(jnp.float32) / 255.0
    places = jnp.arange(knot_count, dtype=jnp.float32)
    scaled = values * (knot_count - 1.0)
    weights = jnp.maximum(0.0, 1.0 - jnp.abs(places[:, None] - scaled[None, :]))
    return jnp.dot(levels, weights, precision=highest, preferred_element_type=jnp.float32)


def classify(density, transfer_table):
    depth_count, rows_y, cells_z = density.shape
    grouped = math.gcd(depth_count, 4)
    blocks = density.reshape(depth_count // grouped, grouped * rows_y * cells_z)
    looked = lax.map(lambda block_cells: lookup(block_cells, transfer_table), blocks)
    looked = looked.reshape(depth_count // grouped, 4, grouped, rows_y, cells_z)
    return looked.transpose(0, 2, 1, 3, 4).reshape(depth_count, 4, rows_y, cells_z)


def emission(classed, shaded, step_len):
    optical = step_len * 2.0 * classed[:, 3]
    opacity = 1.0 - jnp.exp(-optical)
    colour = classed[:, :3] * (shaded * opacity)[:, None]
    return jnp.concatenate([colour, optical[:, None]], axis=1)


def shift_slice(slab, offset):
    framed = jnp.pad(slab, ((0, 0), (0, 0), (SHEAR, SHEAR)))
    return lax.dynamic_slice_in_dim(framed, SHEAR - offset, slab.shape[2], 2)


def ahead_masks(length, turn_flags):
    ranking = jnp.arange(length)
    lower_mask = (ranking[None, :] < ranking[:, None]).astype(jnp.float32)
    return jnp.where(turn_flags[..., None, None] == 0, lower_mask, lower_mask.T)


def brick_images(fields, offsets, turn_flags):

    def one_view(inputs):
        offset_row, turn_flag = inputs
        sheared = jax.vmap(shift_slice)(fields, offset_row)
        depths = sheared[:, 3]
        masking = ahead_masks(fields.shape[0], turn_flag)
        before = jnp.einsum(
            "ji,iyz->jyz", masking, depths, precision=highest, preferred_element_type=jnp.float32
        )
        summed = jnp.sum(depths, axis=0)
        colour = jnp.sum(jnp.exp(-before)[:, None] * sheared[:, :3], axis=0)
        return jnp.concatenate([colour, summed[None]], axis=0)

    return lax.map(one_view, (offsets, turn_flags))


def finish(colour, summed):
    return jnp.concatenate([colour, (1.0 - jnp.exp(-summed))[:, None]], axis=1)


def over_pieces(received, turn_flags):
    masks = ahead_masks(received.shape[2], turn_flags)
    depths = received[:, 3]
    before = jnp.einsum(
        "vji,vipw->vjpw", masks, depths, precision=highest, preferred_element_type=jnp.float32
    )
    summed = jnp.sum(depths, axis=1)
    colour = jnp.sum(jnp.exp(-before)[:, None] * received[:, :3], axis=2)
    return finish(colour, summed)


def compose_x(brick_parts, turn_flags):
    received = lax.all_to_all(
        brick_parts[:, :, None], "gx", split_axis=3, concat_axis=2, tiled=True
    )
    return over_pieces(received, turn_flags)


def compose_y(brick_parts, turn_flags):
    received = lax.all_to_all(
        brick_parts[:, :, None], "gy", split_axis=3, concat_axis=2, tiled=True
    )
    return over_pieces(received, turn_flags)


def local(density, transfer_table, shear_x, shear_y, direction):
    count_x = lax.axis_size("gx")
    count_y = lax.axis_size("gy")
    depth_x, depth_y, cells_z = density.shape
    padded = with_halo(density, (("gx", 0), ("gy", 1)), 1)
    shaded = shading(padded)
    classed = classify(density, transfer_table)
    along_x = emission(classed, shaded, 1.0 / (depth_x * count_x))
    parts_x = brick_images(along_x, shear_x, direction[0])
    image_x = compose_x(parts_x, direction[0])
    along_y = emission(classed, shaded, 1.0 / (depth_y * count_y)).transpose(2, 1, 0, 3)
    parts_y = brick_images(along_y, shear_y, direction[1])
    image_y = compose_y(parts_y, direction[1])
    return (image_x, image_y)


def solution(mesh):
    placed = (P("gx", "gy", None), P(), P(None, "gx"), P(None, "gy"), P())
    return jax.shard_map(
        local,
        mesh=mesh,
        in_specs=placed,
        out_specs=(P(None, None, ("gy", "gx"), None), P(None, None, ("gx", "gy"), None)),
        check_vma=False,
    )
```

profile of v0, /device:TPU:0, one launch (start us, length us, event | category | flops | bytes accessed | tf_op | source)
XLA Modules:
  0.0 407.7 jit_solution(6460592435249260645)
XLA Ops:
  1.4 2.3 collective-permute-start.1
  5.1 1.4 reshape.154
  9.8 87.4 %while.36 = (s32[]{:T(128)}, f32[8,4,32768]{2,1,0:T(4,128)}, f32[4,128]{1,0:T(4,128)S(1)}, f32[8,32768]{1,0:T(8,128)S(1)}, s32[]{:T(128)}) while((s32[]{:T(128)}, f32[8,4,32768]{2,1,0:T(4,128)}, f32[4,128]{1,0:T(4,128)S(1)}, f32[8,32768]{1,0:T(8,128)S(1)}, s32[]{:T(128)}) %tuple.95), condition=%wide.region_1.2_spmd, body=%wide.region_0.1_spmd.sunk | while | flops 218137088 | bytes 919629 | solution.py:52
  9.9 10.8 %fusion.75 = f32[8,4,32768]{2,1,0:T(4,128)} fusion(f32[8,4,32768]{2,1,0:T(4,128)} %get-tuple-element.383, s32[]{:T(128)S(6)} %copy.130, f32[32768]{0:T(1024)S(1)} %bitcast.131, f32[4,128]{1,0:T(4,128)S(1)} %get-tuple-element.389), kind=kOutput, calls=%fused_computation.3.clone.1 | convolution fusion | flops 218104320 | bytes 657412 | tf_op jit(solution)/shard_map/while/body/eval_jaxpr/dot_general | solution.py:45
  20.8 10.8 %fusion.75 = f32[8,4,32768]{2,1,0:T(4,128)} fusion(f32[8,4,32768]{2,1,0:T(4,128)} %get-tuple-element.383, s32[]{:T(128)S(6)} %copy.130, f32[32768]{0:T(1024)S(1)} %bitcast.131, f32[4,128]{1,0:T(4,128)S(1)} %get-tuple-element.389), kind=kOutput, calls=%fused_computation.3.clone.1 | convolution fusion | flops 218104320 | bytes 657412 | tf_op jit(solution)/shard_map/while/body/eval_jaxpr/dot_general | solution.py:45
  31.7 10.8 %fusion.75 = f32[8,4,32768]{2,1,0:T(4,128)} fusion(f32[8,4,32768]{2,1,0:T(4,128)} %get-tuple-element.383, s32[]{:T(128)S(6)} %copy.130, f32[32768]{0:T(1024)S(1)} %bitcast.131, f32[4,128]{1,0:T(4,128)S(1)} %get-tuple-element.389), kind=kOutput, calls=%fused_computation.3.clone.1 | convolution fusion | flops 218104320 | bytes 657412 | tf_op jit(solution)/shard_map/while/body/eval_jaxpr/dot_general | solution.py:45
  42.7 10.8 %fusion.75 = f32[8,4,32768]{2,1,0:T(4,128)} fusion(f32[8,4,32768]{2,1,0:T(4,128)} %get-tuple-element.383, s32[]{:T(128)S(6)} %copy.130, f32[32768]{0:T(1024)S(1)} %bitcast.131, f32[4,128]{1,0:T(4,128)S(1)} %get-tuple-element.389), kind=kOutput, calls=%fused_computation.3.clone.1 | convolution fusion | flops 218104320 | bytes 657412 | tf_op jit(solution)/shard_map/while/body/eval_jaxpr/dot_general | solution.py:45
  53.6 10.8 %fusion.75 = f32[8,4,32768]{2,1,0:T(4,128)} fusion(f32[8,4,32768]{2,1,0:T(4,128)} %get-tuple-element.383, s32[]{:T(128)S(6)} %copy.130, f32[32768]{0:T(1024)S(1)} %bitcast.131, f32[4,128]{1,0:T(4,128)S(1)} %get-tuple-element.389), kind=kOutput, calls=%fused_computation.3.clone.1 | convolution fusion | flops 218104320 | bytes 657412 | tf_op jit(solution)/shard_map/while/body/eval_jaxpr/dot_general | solution.py:45
  64.5 10.8 %fusion.75 = f32[8,4,32768]{2,1,0:T(4,128)} fusion(f32[8,4,32768]{2,1,0:T(4,128)} %get-tuple-element.383, s32[]{:T(128)S(6)} %copy.130, f32[32768]{0:T(1024)S(1)} %bitcast.131, f32[4,128]{1,0:T(4,128)S(1)} %get-tuple-element.389), kind=kOutput, calls=%fused_computation.3.clone.1 | convolution fusion | flops 218104320 | bytes 657412 | tf_op jit(solution)/shard_map/while/body/eval_jaxpr/dot_general | solution.py:45
  75.5 10.8 %fusion.75 = f32[8,4,32768]{2,1,0:T(4,128)} fusion(f32[8,4,32768]{2,1,0:T(4,128)} %get-tuple-element.383, s32[]{:T(128)S(6)} %copy.130, f32[32768]{0:T(1024)S(1)} %bitcast.131, f32[4,128]{1,0:T(4,128)S(1)} %get-tuple-element.389), kind=kOutput, calls=%fused_computation.3.clone.1 | convolution fusion | flops 218104320 | bytes 657412 | tf_op jit(solution)/shard_map/while/body/eval_jaxpr/dot_general | solution.py:45
  86.4 10.8 %fusion.75 = f32[8,4,32768]{2,1,0:T(4,128)} fusion(f32[8,4,32768]{2,1,0:T(4,128)} %get-tuple-element.383, s32[]{:T(128)S(6)} %copy.130, f32[32768]{0:T(1024)S(1)} %bitcast.131, f32[4,128]{1,0:T(4,128)S(1)} %get-tuple-element.389), kind=kOutput, calls=%fused_computation.3.clone.1 | convolution fusion | flops 218104320 | bytes 657412 | tf_op jit(solution)/shard_map/while/body/eval_jaxpr/dot_general | solution.py:45
  97.2 6.1 %reshape.173 = f32[8,4,4,64,128]{4,3,2,1,0:T(8,128)} reshape(f32[8,4,32768]{2,1,0:T(4,128)} %get-tuple-element.184) | data formatting | bytes 8388608 | tf_op jit(solution)/shard_map/reshape | solution.py:53
  103.3 2.6 copy.67
  105.9 1.9 copy-done
  110.0 5.2 %collective-permute-start.3 = (f32[34,1,128]{2,1,0:T(1,128)S(1)}, f32[34,1,128]{2,1,0:T(1,128)S(1)}, u32[]{:S(2)}, u32[]{:S(2)}) collective-permute-start(f32[34,1,128]{2,1,0:T(1,128)S(1)} %get-tuple-element.266), channel_id=1, source_target_pairs={{0,1},{1,2},{2,3},{4,5},{5,6},{6,7},{8,9},{9,10},{10,11},{12,13},{... | collective-permute-start | bytes 52232 | tf_op jit(solution)/shard_map/ppermute | solution.py:22
  117.3 2.7 bitcast_multiply_fusion
  120.5 4.3 %fusion.53 = (f32[64,4,32,128]{3,0,1,2:T(8,128)}, f32[32,4,64,128]{3,2,1,0:T(8,128)}) fusion(f32[32,1,64,128]{3,2,1,0:T(8,128)S(1)} %slice_multiply_fusion.3, f32[32,3,64,128]{3,2,1,0:T(8,128)S(1)} %slice_multiply_fusion.2), kind=kLoop, calls=%fused_computation.113 | loop fusion | flops 1048576 | bytes 12582912 | tf_op jit(solution)/shard_map/transpose | solution.py:131
  124.7 8.7 %copy.68 = f32[32,4,64,128]{2,1,0,3:T(4,128)} copy(f32[32,4,64,128]{3,2,1,0:T(8,128)} %get-tuple-element.265) | data formatting | bytes 8388608 | tf_op jit(solution)/shard_map/while | solution.py:89
  133.4 14.6 %copy.74 = f32[64,4,32,128]{2,1,0,3:T(4,128)} copy(f32[64,4,32,128]{3,0,1,2:T(8,128)} %get-tuple-element.264) | data formatting | bytes 8388608 | tf_op jit(solution)/shard_map/while | solution.py:89
  148.0 140.8 %while.38 = (s32[]{:T(128)}, f32[2,4,32,128]{3,1,0,2:T(4,128)}, s32[2]{0:T(128)S(1)}, f32[64,4,32,128]{2,1,0,3:T(4,128)}, s32[2,64]{1,0:T(2,128)S(1)}, /*index=5*/s32[]{:T(128)}, f32[]{:T(128)}, s32[1]{0:T(128)}) while((s32[]{:T(128)}, f32[2,4,32,128]{3,1,0,2:T(4,128)}, s32[2]{0:T(128)S(1)}, f32[64,4,32,128]{2,1,0,3:T(4,128)}, ...), condition=%wide.region_11.12_spmd, body=%wide.region_8.11_spmd.sunk | while | flops 203444800 | bytes 30869116 | solution.py:89
  148.0 15.2 %pad.119 = f32[64,4,32,160]{2,1,0,3:T(4,128)} pad(f32[64,4,32,128]{2,1,0,3:T(4,128)} %get-tuple-element.435, f32[]{:T(128)} %constant.130.clone.3..sunk.1), padding=0_0x0_0x0_0x16_16 | pad | bytes 9437188 | tf_op jit(solution)/shard_map/while/body/eval_jaxpr/vmap(jit(_pad))/pad | solution.py:65
  163.2 23.4 %gather_fusion.1 = f32[64,4,32,128]{2,1,3,0:T(4,128)} fusion(f32[64,4,32,160]{2,1,0,3:T(4,128)} %pad.119, s32[64]{0:T(128)S(1)} %or_bitcast_fusion.5), kind=kCustom, calls=%fused_computation.1.clone.1 | custom fusion | bytes 8389632 | tf_op jit(solution)/shard_map/while/body/eval_jaxpr/vmap()/gather | solution.py:66
  186.7 9.7 %fusion.83 = (f32[64,1,32,128]{2,1,3,0:T(1,128)}, f32[32,128]{0,1:T(8,128)S(1)}) fusion(f32[64,4,32,128]{2,1,3,0:T(4,128)} %gather_fusion.1), kind=kLoop, calls=%fused_computation.115.clone.1 | loop fusion | flops 258048 | bytes 2113536 | tf_op jit(solution)/shard_map/while/body/eval_jaxpr/slice | solution.py:80
  196.4 5.3 %copy.122 = f32[64,1,32,128]{3,0,2,1:T(8,128)S(1)} copy(f32[64,1,32,128]{2,1,3,0:T(1,128)} %get-tuple-element.376) | data formatting | bytes 2097152 | tf_op jit(solution)/shard_map/while
  204.0 2.7 copy.123
  206.7 10.9 %fusion.85 = f32[3,32,128]{1,0,2:T(4,128)S(1)} fusion(f32[64,4,32,128]{2,1,3,0:T(4,128)} %gather_fusion.1, f32[64,32,128]{1,2,0:T(8,128)} %copy.123), kind=kLoop, calls=%fused_computation.37.clone.1 | loop fusion | flops 1560576 | bytes 4243456 | tf_op jit(solution)/shard_map/while/body/eval_jaxpr/reduce_sum | solution.py:86
  218.4 15.2 %pad.119 = f32[64,4,32,160]{2,1,0,3:T(4,128)} pad(f32[64,4,32,128]{2,1,0,3:T(4,128)} %get-tuple-element.435, f32[]{:T(128)} %constant.130.clone.3..sunk.1), padding=0_0x0_0x0_0x16_16 | pad | bytes 9437188 | tf_op jit(solution)/shard_map/while/body/eval_jaxpr/vmap(jit(_pad))/pad | solution.py:65
  233.6 23.4 %gather_fusion.1 = f32[64,4,32,128]{2,1,3,0:T(4,128)} fusion(f32[64,4,32,160]{2,1,0,3:T(4,128)} %pad.119, s32[64]{0:T(128)S(1)} %or_bitcast_fusion.5), kind=kCustom, calls=%fused_computation.1.clone.1 | custom fusion | bytes 8389632 | tf_op jit(solution)/shard_map/while/body/eval_jaxpr/vmap()/gather | solution.py:66
  257.1 9.7 %fusion.83 = (f32[64,1,32,128]{2,1,3,0:T(1,128)}, f32[32,128]{0,1:T(8,128)S(1)}) fusion(f32[64,4,32,128]{2,1,3,0:T(4,128)} %gather_fusion.1), kind=kLoop, calls=%fused_computation.115.clone.1 | loop fusion | flops 258048 | bytes 2113536 | tf_op jit(solution)/shard_map/while/body/eval_jaxpr/slice | solution.py:80
  266.8 5.3 %copy.122 = f32[64,1,32,128]{3,0,2,1:T(8,128)S(1)} copy(f32[64,1,32,128]{2,1,3,0:T(1,128)} %get-tuple-element.376) | data formatting | bytes 2097152 | tf_op jit(solution)/shard_map/while
  274.4 2.7 copy.123
  277.1 10.9 %fusion.85 = f32[3,32,128]{1,0,2:T(4,128)S(1)} fusion(f32[64,4,32,128]{2,1,3,0:T(4,128)} %gather_fusion.1, f32[64,32,128]{1,2,0:T(8,128)} %copy.123), kind=kLoop, calls=%fused_computation.37.clone.1 | loop fusion | flops 1560576 | bytes 4243456 | tf_op jit(solution)/shard_map/while/body/eval_jaxpr/reduce_sum | solution.py:86
  288.8 6.0 %all-to-all-start.1 = ((f32[2,4,1,32,128]{4,1,0,2,3:T(4,128)}), f32[2,4,1,32,128]{4,1,0,2,3:T(4,128)S(1)}, u32[]{:S(2)}, u32[]{:S(2)}) async-start(f32[2,4,1,32,128]{4,1,0,2,3:T(4,128)} %bitcast.34), calls=%async_computation.1 | async-start | bytes 262144 | tf_op jit(solution)/shard_map/all_to_all | solution.py:115
  294.9 98.4 %while.37 = (s32[]{:T(128)}, f32[2,4,64,128]{3,1,0,2:T(4,128)}, s32[2]{0:T(128)S(1)}, f32[32,4,64,128]{2,1,0,3:T(4,128)}, s32[2,32]{1,0:T(2,128)S(1)}, /*index=5*/s32[]{:T(128)}, f32[]{:T(128)}, s32[1]{0:T(128)}) while((s32[]{:T(128)}, f32[2,4,64,128]{3,1,0,2:T(4,128)}, s32[2]{0:T(128)S(1)}, f32[32,4,64,128]{2,1,0,3:T(4,128)}, ...), condition=%wide.region_5.6_spmd, body=%wide.region_2.5_spmd.sunk | while | flops 102765856 | bytes 33424308 | solution.py:89
  304.2 11.6 %pad.116 = f32[32,4,64,160]{2,1,0,3:T(4,128)} pad(f32[32,4,64,128]{2,1,0,3:T(4,128)} %get-tuple-element.411, f32[]{:T(128)} %constant.130.clone.3..sunk), padding=0_0x0_0x0_0x16_16 | pad | bytes 9437188 | tf_op jit(solution)/shard_map/while/body/eval_jaxpr/vmap(jit(_pad))/pad | solution.py:65
  315.9 13.5 %gather_fusion = f32[32,4,64,128]{2,1,3,0:T(4,128)} fusion(f32[32,4,64,160]{2,1,0,3:T(4,128)} %pad.116, s32[32]{0:T(128)S(1)} %or_bitcast_fusion.4), kind=kCustom, calls=%fused_computation.clone.1 | custom fusion | bytes 8389120 | tf_op jit(solution)/shard_map/while/body/eval_jaxpr/vmap()/gather | solution.py:66
  329.4 6.6 %fusion.78 = (f32[32,1,64,128]{2,1,3,0:T(1,128)S(1)}, f32[64,128]{0,1:T(8,128)S(1)}) fusion(f32[32,4,64,128]{2,1,3,0:T(4,128)} %gather_fusion), kind=kLoop, calls=%fused_computation.114.clone.1 | loop fusion | flops 253952 | bytes 2129920 | tf_op jit(solution)/shard_map/while/body/eval_jaxpr/slice | solution.py:80
  338.3 2.0 fusion.79
  340.3 1.8 copy.118
  342.2 5.5 %fusion.80 = f32[3,64,128]{1,0,2:T(4,128)S(1)} fusion(f32[32,4,64,128]{2,1,3,0:T(4,128)} %gather_fusion, f32[32,64,128]{1,2,0:T(8,128)S(1)} %copy.118), kind=kLoop, calls=%fused_computation.19.clone.1 | loop fusion | flops 1548288 | bytes 4292608 | tf_op jit(solution)/shard_map/while/body/eval_jaxpr/reduce_sum | solution.py:86
  348.7 11.6 %pad.116 = f32[32,4,64,160]{2,1,0,3:T(4,128)} pad(f32[32,4,64,128]{2,1,0,3:T(4,128)} %get-tuple-element.411, f32[]{:T(128)} %constant.130.clone.3..sunk), padding=0_0x0_0x0_0x16_16 | pad | bytes 9437188 | tf_op jit(solution)/shard_map/while/body/eval_jaxpr/vmap(jit(_pad))/pad | solution.py:65
  360.4 13.5 %gather_fusion = f32[32,4,64,128]{2,1,3,0:T(4,128)} fusion(f32[32,4,64,160]{2,1,0,3:T(4,128)} %pad.116, s32[32]{0:T(128)S(1)} %or_bitcast_fusion.4), kind=kCustom, calls=%fused_computation.clone.1 | custom fusion | bytes 8389120 | tf_op jit(solution)/shard_map/while/body/eval_jaxpr/vmap()/gather | solution.py:66
  373.9 6.6 %fusion.78 = (f32[32,1,64,128]{2,1,3,0:T(1,128)S(1)}, f32[64,128]{0,1:T(8,128)S(1)}) fusion(f32[32,4,64,128]{2,1,3,0:T(4,128)} %gather_fusion), kind=kLoop, calls=%fused_computation.114.clone.1 | loop fusion | flops 253952 | bytes 2129920 | tf_op jit(solution)/shard_map/while/body/eval_jaxpr/slice | solution.py:80
  382.8 2.0 fusion.79
  384.8 1.8 copy.118
  386.7 5.5 %fusion.80 = f32[3,64,128]{1,0,2:T(4,128)S(1)} fusion(f32[32,4,64,128]{2,1,3,0:T(4,128)} %gather_fusion, f32[32,64,128]{1,2,0:T(8,128)S(1)} %copy.118), kind=kLoop, calls=%fused_computation.19.clone.1 | loop fusion | flops 1548288 | bytes 4292608 | tf_op jit(solution)/shard_map/while/body/eval_jaxpr/reduce_sum | solution.py:86
  393.3 6.3 %all-to-all-start = ((f32[2,4,1,64,128]{4,1,0,2,3:T(4,128)}), f32[2,4,1,64,128]{4,1,0,2,3:T(4,128)S(1)}, u32[]{:S(2)}, u32[]{:S(2)}) async-start(f32[2,4,1,64,128]{4,1,0,2,3:T(4,128)} %bitcast.137), calls=%async_computation | async-start | bytes 524288 | tf_op jit(solution)/shard_map/all_to_all | solution.py:108
  400.6 5.9 %all-to-all-done = f32[2,4,1,64,128]{4,1,0,2,3:T(4,128)S(1)} async-done(((f32[2,4,1,64,128]{4,1,0,2,3:T(4,128)}), f32[2,4,1,64,128]{4,1,0,2,3:T(4,128)S(1)}, u32[]{:S(2)}, u32[]{:S(2)}) %all-to-all-start) | async-done | bytes 262176 | tf_op jit(solution)/shard_map/all_to_all | solution.py:108
  (102 shorter events, 23.4 us)
Async XLA Ops:
  1.4 107.1 %collective-permute-start.1 = (f32[1,64,128]{2,1,0:T(8,128)S(1)}, f32[1,64,128]{2,1,0:T(8,128)S(1)}, u32[]{:S(2)}, u32[]{:S(2)}) collective-permute-start(f32[1,64,128]{2,1,0:T(8,128)S(1)} %get-tuple-element.269), channel_id=1, source_target_pairs={{0,4},{4,8},{8,12},{12,16},{16,20},{20,24},{24,28},{1,5},{5,9},{9,... | collective-permute-start | bytes 98312 | tf_op jit(solution)/shard_map/ppermute | solution.py:22
  3.8 104.9 %collective-permute-start = (f32[1,64,128]{2,1,0:T(8,128)S(1)}, f32[1,64,128]{2,1,0:T(8,128)S(1)}, u32[]{:S(2)}, u32[]{:S(2)}) collective-permute-start(f32[1,64,128]{2,1,0:T(8,128)S(1)} %get-tuple-element.268), channel_id=1, source_target_pairs={{4,0},{8,4},{12,8},{16,12},{20,16},{24,20},{28,24},{5,1},{9,5},{13... | collective-permute-start | bytes 98312 | tf_op jit(solution)/shard_map/ppermute | solution.py:25
  103.3 5.3 %copy-start.2 = (f32[32,64,128]{2,1,0:T(8,128)S(1)}, f32[32,64,128]{2,1,0:T(8,128)}, u32[]{:S(2)}) copy-start(f32[32,64,128]{2,1,0:T(8,128)} %param.11) | copy-start | bytes 3145732
  105.9 2.0 copy-start
  108.7 7.1 %collective-permute-start.2 = (f32[34,1,128]{2,1,0:T(1,128)S(1)}, f32[34,1,128]{2,1,0:T(1,128)S(1)}, u32[]{:S(2)}, u32[]{:S(2)}) collective-permute-start(f32[34,1,128]{2,1,0:T(1,128)S(1)} %get-tuple-element.267), channel_id=1, source_target_pairs={{1,0},{2,1},{3,2},{5,4},{6,5},{7,6},{9,8},{10,9},{11,10},{13,12},{... | collective-permute-start | bytes 52232 | tf_op jit(solution)/shard_map/ppermute | solution.py:25
  110.0 6.4 %collective-permute-start.3 = (f32[34,1,128]{2,1,0:T(1,128)S(1)}, f32[34,1,128]{2,1,0:T(1,128)S(1)}, u32[]{:S(2)}, u32[]{:S(2)}) collective-permute-start(f32[34,1,128]{2,1,0:T(1,128)S(1)} %get-tuple-element.266), channel_id=1, source_target_pairs={{0,1},{1,2},{2,3},{4,5},{5,6},{6,7},{8,9},{9,10},{10,11},{12,13},{... | collective-permute-start | bytes 52232 | tf_op jit(solution)/shard_map/ppermute | solution.py:22
  115.8 4.1 %copy-start.1 = (f32[8,4,4,64,128]{4,3,2,1,0:T(8,128)S(1)}, f32[8,4,4,64,128]{4,3,2,1,0:T(8,128)}, u32[]{:S(2)}) copy-start(f32[8,4,4,64,128]{4,3,2,1,0:T(8,128)} %copy-done) | copy-start | bytes 12582916
  133.4 14.6 %copy-start.12 = (s32[2,64]{1,0:T(2,128)S(1)}, s32[2,64]{1,0:T(2,128)}, u32[]{:S(2)}) copy-start(s32[2,64]{1,0:T(2,128)} %param.14) | copy-start | bytes 1540
  148.0 146.8 %copy-start.11 = (s32[2]{0:T(128)S(1)}, s32[2]{0:T(128)}, u32[]{:S(2)}) copy-start(s32[2]{0:T(128)} %get-tuple-element.394) | copy-start | bytes 28
  148.0 146.8 %copy-start.13 = (s32[2,32]{1,0:T(2,128)S(1)}, s32[2,32]{1,0:T(2,128)}, u32[]{:S(2)}) copy-start(s32[2,32]{1,0:T(2,128)} %param.13) | copy-start | bytes 772
  288.8 104.5 %all-to-all-start.1 = ((f32[2,4,1,32,128]{4,1,0,2,3:T(4,128)}), f32[2,4,1,32,128]{4,1,0,2,3:T(4,128)S(1)}, u32[]{:S(2)}, u32[]{:S(2)}) async-start(f32[2,4,1,32,128]{4,1,0,2,3:T(4,128)} %bitcast.34), calls=%async_computation.1 | async-start | bytes 262144 | tf_op jit(solution)/shard_map/all_to_all | solution.py:115
  294.8 104.8 %copy-start.7 = (f32[4,4]{1,0:T(4,128)S(1)}, f32[4,4]{1,0:T(4,128)}, u32[]{:S(2)}) copy-start(f32[4,4]{1,0:T(4,128)} %get-tuple-element.280) | copy-start | bytes 196
  294.8 104.8 %copy-start.8 = (f32[4,4]{1,0:T(4,128)S(1)}, f32[4,4]{1,0:T(4,128)}, u32[]{:S(2)}) copy-start(f32[4,4]{1,0:T(4,128)} %get-tuple-element.281) | copy-start | bytes 196
  294.9 104.8 %copy-start.10 = (pred[2]{0:T(512)(128)(4,1)S(1)}, pred[2]{0:T(512)(128)(4,1)}, u32[]{:S(2)}) copy-start(pred[2]{0:T(512)(128)(4,1)} %get-tuple-element.274) | copy-start | bytes 10
  294.9 111.7 %copy-start.5 = (f32[8,8]{1,0:T(8,128)S(1)}, f32[8,8]{1,0:T(8,128)}, u32[]{:S(2)}) copy-start(f32[8,8]{1,0:T(8,128)} %get-tuple-element.278) | copy-start | bytes 772
  294.9 111.7 %copy-start.6 = (f32[8,8]{1,0:T(8,128)S(1)}, f32[8,8]{1,0:T(8,128)}, u32[]{:S(2)}) copy-start(f32[8,8]{1,0:T(8,128)} %get-tuple-element.279) | copy-start | bytes 772
  294.9 111.7 %copy-start.9 = (pred[2]{0:T(512)(128)(4,1)S(1)}, pred[2]{0:T(512)(128)(4,1)}, u32[]{:S(2)}) copy-start(pred[2]{0:T(512)(128)(4,1)} %get-tuple-element.275) | copy-start | bytes 10
  342.2 5.8 %copy-start.3 = (f32[2,4,64,128]{3,1,0,2:T(4,128)S(1)}, f32[2,4,64,128]{3,1,0,2:T(4,128)}, u32[]{:S(2)}) copy-start(f32[2,4,64,128]{3,1,0,2:T(4,128)} %get-tuple-element.401) | copy-start | bytes 786436 | tf_op jit(solution)/shard_map/while
  348.0 0.7 copy-start.4
  386.7 5.8 %copy-start.3 = (f32[2,4,64,128]{3,1,0,2:T(4,128)S(1)}, f32[2,4,64,128]{3,1,0,2:T(4,128)}, u32[]{:S(2)}) copy-start(f32[2,4,64,128]{3,1,0,2:T(4,128)} %get-tuple-element.401) | copy-start | bytes 786436 | tf_op jit(solution)/shard_map/while
  392.6 0.7 copy-start.4
  393.3 13.2 %all-to-all-start = ((f32[2,4,1,64,128]{4,1,0,2,3:T(4,128)}), f32[2,4,1,64,128]{4,1,0,2,3:T(4,128)S(1)}, u32[]{:S(2)}, u32[]{:S(2)}) async-start(f32[2,4,1,64,128]{4,1,0,2,3:T(4,128)} %bitcast.137), calls=%async_computation | async-start | bytes 524288 | tf_op jit(solution)/shard_map/all_to_all | solution.py:108
where the time goes:
time: 414 us; the launch traced here: 408 us
  local copies, waits for them, and re-layouts  193 us (47%)
  matrix products  93.1 us (22%)
  other arithmetic  79.7 us (19%)
  starting transfers between devices  22.4 us (5%)
  loops' own time  12.1 us (3%)
  waiting for transfers between devices  6.52 us (2%)
    dot_general x8, matrix products, lookup(): jnp.dot(levels, weights, precision=highest, preferred_element_type=jnp.fl...  86.4 us
    gather x4, local copies, waits for them, and re-layouts, shift_slice(): return lax.dynamic_slice_in_dim(framed, SHEAR - offset, slab.shape[2], 2)  73.9 us
    pad x4, local copies, waits for them, and re-layouts, shift_slice(): framed = jnp.pad(slab, ((0, 0), (0, 0), (SHEAR, SHEAR)))  53.7 us
    reduce_sum x4, other arithmetic, one_view(): colour = jnp.sum(jnp.exp(-before)[:, None] * sheared[:, :3], axis=0)  32.9 us
    slice x4, other arithmetic, one_view(): depths = sheared[:, 3]  32.6 us
    while x2, local copies, waits for them, and re-layouts, brick_images(): return lax.map(one_view, (offsets, turn_flags))  23.3 us
    while x14, local copies, waits for them, and re-layouts  14.2 us
    another operation x2, loops' own time, brick_images(): return lax.map(one_view, (offsets, turn_flags))  12.1 us
  transfers between devices with their start and end apart: 6, of which 2 were waited for; matrix products, arithmetic and copies ran while one was open for 46% of the time, Pallas kernels for 0%

commit v1 on v0

v1 whole, which is shorter than its diff:
```python
import functools
import math

import jax
import jax.numpy as jnp
from jax import lax
from jax.experimental import pallas as pl
from jax.experimental.pallas import tpu as pltpu
from jax.sharding import PartitionSpec as P

MESH = pl.DeviceIdType.MESH
LOG2E = math.log2(math.e)
UNROLL = 4


def take(row, places):
    return jnp.take_along_axis(
        jnp.broadcast_to(row, places.shape), places, axis=1, mode="promise_in_bounds"
    )


def exchange_copy(parts, received, send_sem, recv_sem, axis, me, count, step):
    target = lax.rem(me + step, count)
    return pltpu.make_async_remote_copy(
        src_ref=parts.at[target],
        dst_ref=received.at[me],
        send_sem=send_sem.at[step],
        recv_sem=recv_sem.at[step],
        device_id={axis: target},
        device_id_type=MESH,
    )


def march(fields, shear_ref, direction_ref, family, view, depth, pitch, begin, rows, cells_z):
    lanes = lax.broadcasted_iota(jnp.int32, (rows, cells_z), 1)
    turned = direction_ref[family, view]

    def step(i, carried):
        behind, colours = carried
        place = jnp.where(turned == 0, i, depth - 1 - i)
        shift = shear_ref[view, place]
        amount = jnp.where(shift < 0, shift + cells_z, shift)
        inside = (lanes >= shift) & (lanes < cells_z + shift)
        at = pl.ds(pl.multiple_of(place * pitch + begin, 8), rows)
        sheared = [pltpu.roll(fields[c, at, :], amount, 1) for c in range(4)]
        through = jnp.where(inside, jnp.exp2(-behind), 0.0)
        colours = tuple(total + through * sheared[c] for c, total in enumerate(colours))
        return behind + jnp.where(inside, sheared[3], 0.0), colours

    zero = jnp.zeros((rows, cells_z), jnp.float32)
    return lax.fori_loop(0, depth, step, (zero, (zero, zero, zero)), unroll=UNROLL)


def compose(received, direction_ref, family, count, views, out_ref):
    for view in range(views):
        turned = direction_ref[family, view].astype(jnp.float32)
        depths = [received[i, view * 4 + 3] for i in range(count)]
        lower, upper = [jnp.zeros_like(depths[0])], [jnp.zeros_like(depths[0])]
        for i in range(count):
            lower.append(lower[-1] + depths[i])
            upper.append(upper[-1] + depths[count - 1 - i])
        through = [
            jnp.exp2(-(lower[i] * (1.0 - turned) + upper[count - 1 - i] * turned))
            for i in range(count)
        ]
        for c in range(3):
            total = through[0] * received[0, view * 4 + c]
            for i in range(1, count):
                total += through[i] * received[i, view * 4 + c]
            out_ref[view, c] = total
        out_ref[view, 3] = 1.0 - jnp.exp2(-lower[-1])


def halo_kernel(
    dims, counts, density,
    halo_x_low, halo_x_high, halo_y_low, halo_y_high, face_low, face_high, halo_send, halo_recv,
):
    depth_x, depth_y, cells_z = dims
    count_x, count_y = counts
    me_x, me_y = lax.axis_index("gx"), lax.axis_index("gy")

    last = (depth_x - 1) * depth_y
    halos = []
    barrier = pltpu.get_barrier_semaphore()
    for k, (axis, me, count, delta, src, dst) in enumerate((
        ("gx", me_x, count_x, 1, density.at[pl.ds(last, depth_y), :], halo_x_low),
        ("gx", me_x, count_x, -1, density.at[pl.ds(0, depth_y), :], halo_x_high),
        ("gy", me_y, count_y, 1, face_high, halo_y_low),
        ("gy", me_y, count_y, -1, face_low, halo_y_high),
    )):
        partner = {axis: lax.rem(me + delta + count, count)}
        copy = pltpu.make_async_remote_copy(
            src_ref=src, dst_ref=dst, send_sem=halo_send.at[k], recv_sem=halo_recv.at[k],
            device_id=partner, device_id_type=MESH,
        )
        sends = me < count - 1 if delta == 1 else me > 0
        receives = me > 0 if delta == 1 else me < count - 1
        halos.append((copy, sends, receives, dst))

        @pl.when(sends)
        def _():
            pl.semaphore_signal(barrier, inc=1, device_id=partner, device_id_type=MESH)

    face_low[...] = density[pl.ds(0, depth_x, stride=depth_y), :]
    face_high[...] = density[pl.ds(depth_y - 1, depth_x, stride=depth_y), :]
    pl.semaphore_wait(barrier, sum(sends.astype(jnp.int32) for _, sends, _, _ in halos))

    for copy, sends, receives, dst in halos:
        pl.when(sends)(copy.start)

        @pl.when(jnp.logical_not(receives))
        def _():
            dst[...] = jnp.zeros_like(dst)

    for copy, sends, receives, dst in halos:
        pl.when(receives)(copy.wait_recv)
        pl.when(sends)(copy.wait_send)


def brick_kernel(
    dims, counts,
    density, table, shear_x, shear_y, direction,
    halo_x_low, halo_x_high, halo_y_low, halo_y_high,
    parts_x, parts_y, fields_x, fields_y,
):
    depth_x, depth_y, cells_z = dims
    count_x, count_y = counts
    views = shear_x.shape[0]
    knots = table.shape[1]

    step_x = 2.0 * LOG2E / (depth_x * count_x)
    step_y = 2.0 * LOG2E / (depth_y * count_y)
    levels = table[...].astype(jnp.float32) * (1.0 / 255.0)
    rises = pltpu.roll(levels, knots - 1, 1) - levels

    def classify(x, _):
        at = pl.ds(pl.multiple_of(x * depth_y, 8), depth_y)
        scaled = density[at, :] * (knots - 1.0)
        places = jnp.minimum(scaled.astype(jnp.int32), knots - 1)
        rest = scaled - places.astype(jnp.float32)
        for c in range(4):
            value = take(levels[c:c + 1], places) + rest * take(rises[c:c + 1], places)
            if c < 3:
                fields_x[c, at, :] = value
            else:
                fields_x[c, at, :] = value * step_x
                fields_y[c, pl.ds(x, depth_y, stride=depth_x), :] = value * step_y
        return 0

    lax.fori_loop(0, depth_x, classify, 0)

    lanes = lax.broadcasted_iota(jnp.int32, (depth_y, cells_z), 1)
    ranks = lax.broadcasted_iota(jnp.int32, (depth_y, cells_z), 0)

    def shade(x, before, here, after):
        low = halo_y_low[pl.ds(x, 1), :]
        high = halo_y_high[pl.ds(x, 1), :]
        rise_x = after - before
        rise_y = jnp.where(ranks == depth_y - 1, high, pltpu.roll(here, depth_y - 1, 0)) - jnp.where(
            ranks == 0, low, pltpu.roll(here, 1, 0)
        )
        rise_z = jnp.where(lanes == cells_z - 1, 0.0, pltpu.roll(here, cells_z - 1, 1)) - jnp.where(
            lanes == 0, 0.0, pltpu.roll(here, 1, 1)
        )
        facing = jnp.abs(rise_x + 2.0 * (rise_y + rise_z)) * (0.7 / 3.0)
        steep = rise_x * rise_x + rise_y * rise_y + rise_z * rise_z + 0.04
        shaded = 0.3 + facing * lax.rsqrt(steep)
        at = pl.ds(pl.multiple_of(x * depth_y, 8), depth_y)
        turned_at = pl.ds(x, depth_y, stride=depth_x)
        optical = fields_x[3, at, :]
        gain_x = shaded * (1.0 - jnp.exp2(-optical))
        if step_x == step_y:
            gain_y = gain_x
        else:
            gain_y = shaded * (1.0 - jnp.exp2(-(optical * (step_y / step_x))))
        for c in range(3):
            colour = fields_x[c, at, :]
            fields_x[c, at, :] = colour * gain_x
            fields_y[c, turned_at, :] = colour * gain_y

    def plane(x):
        return density[pl.ds(pl.multiple_of(x * depth_y, 8), depth_y), :]

    def shade_inner(x, _):
        shade(x, plane(x - 1), plane(x), plane(x + 1))
        return 0

    shade(0, halo_x_low[...], plane(0), plane(1))
    lax.fori_loop(1, depth_x - 1, shade_inner, 0)
    shade(depth_x - 1, plane(depth_x - 2), plane(depth_x - 1), halo_x_high[...])

    for fields, shear, family, count, depth, across, parts in (
        (fields_x, shear_x, 0, count_x, depth_x, depth_y, parts_x),
        (fields_y, shear_y, 1, count_y, depth_y, depth_x, parts_y),
    ):
        piece = across // count
        rows = math.gcd(across, 32)
        for view in range(views):
            for begin in range(0, across, rows):
                behind, colours = march(
                    fields, shear, direction, family, view, depth, across, begin, rows, cells_z
                )
                for c, result in enumerate(colours + (behind,)):
                    for r in range(0, rows, piece):
                        parts[(begin + r) // piece, view * 4 + c] = result[r:r + piece]


def compose_kernel(
    counts, views, direction, parts_x, parts_y,
    image_x, image_y, got_x, got_y, send_x, recv_x, send_y, recv_y,
):
    count_x, count_y = counts
    me_x, me_y = lax.axis_index("gx"), lax.axis_index("gy")
    barrier = pltpu.get_barrier_semaphore()
    for axis, me, count in (("gx", me_x, count_x), ("gy", me_y, count_y)):
        for step in range(1, count):
            pl.semaphore_signal(
                barrier, inc=1, device_id={axis: lax.rem(me + step, count)}, device_id_type=MESH
            )
    got_x[me_x] = parts_x[me_x]
    got_y[me_y] = parts_y[me_y]
    pl.semaphore_wait(barrier, count_x + count_y - 2)
    groups = []
    for axis, me, count, parts, got, send, recv in (
        ("gx", me_x, count_x, parts_x, got_x, send_x, recv_x),
        ("gy", me_y, count_y, parts_y, got_y, send_y, recv_y),
    ):
        groups.append([
            exchange_copy(parts, got, send, recv, axis, me, count, step) for step in range(1, count)
        ])
        for copy in groups[-1]:
            copy.start()
    for group, family, count, got, image in (
        (groups[1], 1, count_y, got_y, image_y),
        (groups[0], 0, count_x, got_x, image_x),
    ):
        for copy in group:
            copy.wait_recv()
        compose(got, direction, family, count, views, image)
    for group in groups:
        for copy in group:
            copy.wait_send()


def local(density, transfer_table, shear_x, shear_y, direction):
    count_x, count_y = lax.axis_size("gx"), lax.axis_size("gy")
    counts = (count_x, count_y)
    dims = density.shape
    depth_x, depth_y, cells_z = dims
    views = shear_x.shape[0]
    f32 = jnp.float32
    piece_x, piece_y = depth_y // count_x, depth_x // count_y
    cells = depth_x * depth_y
    vmem = pl.BlockSpec(memory_space=pltpu.VMEM)
    smem = pl.BlockSpec(memory_space=pltpu.SMEM)
    density = density.reshape(cells, cells_z)
    layer_x = jax.ShapeDtypeStruct((depth_y, cells_z), f32)
    layer_y = jax.ShapeDtypeStruct((depth_x, cells_z), f32)
    halos = pl.pallas_call(
        functools.partial(halo_kernel, dims, counts),
        out_shape=(layer_x, layer_x, layer_y, layer_y),
        in_specs=[vmem],
        out_specs=(vmem,) * 4,
        scratch_shapes=[
            pltpu.VMEM((depth_x, cells_z), f32),
            pltpu.VMEM((depth_x, cells_z), f32),
            pltpu.SemaphoreType.DMA((4,)),
            pltpu.SemaphoreType.DMA((4,)),
        ],
        compiler_params=pltpu.CompilerParams(collective_id=0, has_side_effects=True),
    )(density)
    parts = pl.pallas_call(
        functools.partial(brick_kernel, dims, counts),
        out_shape=(
            jax.ShapeDtypeStruct((count_x, views * 4, piece_x, cells_z), f32),
            jax.ShapeDtypeStruct((count_y, views * 4, piece_y, cells_z), f32),
        ),
        in_specs=[vmem, vmem, smem, smem, smem] + [vmem] * 4,
        out_specs=(vmem, vmem),
        scratch_shapes=[
            pltpu.VMEM((4, cells, cells_z), f32),
            pltpu.VMEM((4, cells, cells_z), f32),
        ],
        compiler_params=pltpu.CompilerParams(vmem_limit_bytes=40 * 2**20),
    )(density, transfer_table, shear_x, shear_y, direction, *halos)
    return tuple(pl.pallas_call(
        functools.partial(compose_kernel, counts, views),
        out_shape=(
            jax.ShapeDtypeStruct((views, 4, piece_x, cells_z), f32),
            jax.ShapeDtypeStruct((views, 4, piece_y, cells_z), f32),
        ),
        in_specs=[smem, vmem, vmem],
        out_specs=(vmem, vmem),
        scratch_shapes=[
            pltpu.VMEM((count_x, views * 4, piece_x, cells_z), f32),
            pltpu.VMEM((count_y, views * 4, piece_y, cells_z), f32),
            pltpu.SemaphoreType.DMA((count_x,)),
            pltpu.SemaphoreType.DMA((count_x,)),
            pltpu.SemaphoreType.DMA((count_y,)),
            pltpu.SemaphoreType.DMA((count_y,)),
        ],
        compiler_params=pltpu.CompilerParams(collective_id=1, has_side_effects=True),
    )(direction, *parts))


def solution(mesh):
    placed = (P("gx", "gy", None), P(), P(None, "gx"), P(None, "gy"), P())
    return jax.shard_map(
        local,
        mesh=mesh,
        in_specs=placed,
        out_specs=(P(None, None, ("gy", "gx"), None), P(None, None, ("gx", "gy"), None)),
        check_vma=False,
    )
```

time: 414 us -> 50.5 us (0.12); the launches traced: 408 us -> 50 us
  local copies, waits for them, and re-layouts: 193 us -> 6.96 us
  matrix products: 93.1 us -> 0 us
  other arithmetic: 79.7 us -> 0 us
  Pallas kernels: 0 us -> 42.3 us
  starting transfers between devices: 22.4 us -> 0 us
  loops' own time: 12.1 us -> 0 us
  waiting for transfers between devices: 6.52 us -> 0 us
    dot_general x14 -> x0, matrix products: 93.1 us -> none  [the longest x8 86.4 us: lookup(): jnp.dot(levels, weights, precision=highest, preferred_element_type=jnp.fl...]
    gather x4 -> x0, local copies, waits for them, and re-layouts: 73.9 us -> none  [shift_slice(): return lax.dynamic_slice_in_dim(framed, SHEAR - offset, slab.shape[2], 2)]
    pad x4 -> x0, local copies, waits for them, and re-layouts: 53.7 us -> none  [shift_slice(): framed = jnp.pad(slab, ((0, 0), (0, 0), (SHEAR, SHEAR)))]
    pallas_call x0 -> x3, Pallas kernels: none -> 42.3 us  [the longest x1 24.3 us: local(): pl.pallas_call(functools.partial(brick_kernel, dims, counts), out_shape=(...]
    while x16 -> x0, local copies, waits for them, and re-layouts: 37.4 us -> none  [the longest x2 23.3 us: brick_images(): return lax.map(one_view, (offsets, turn_flags))]
    reduce_sum x6 -> x0, other arithmetic: 32.9 us -> none  [the longest x4 32.9 us: one_view(): colour = jnp.sum(jnp.exp(-before)[:, None] * sheared[:, :3], axis=0)]
    slice x6 -> x0, other arithmetic: 32.6 us -> none  [the longest x4 32.6 us: one_view(): depths = sheared[:, 3]]
    all_to_all x2 -> x0, starting transfers between devices: 12.3 us -> none  [the longest x1 6.26 us: compose_x(): lax.all_to_all(brick_parts[:, :, None], 'gx', split_axis=3, concat_axis=2...]
  transfers between devices with their start and end apart: 6 -> 0, of which waited for: 2 -> 0; matrix products, arithmetic and copies ran while one was open for 46% -> 0% of each run, Pallas kernels for 0% -> 0%
where the time goes in v1:
time: 50.5 us; the launch traced here: 50 us
  Pallas kernels  42.3 us (84%)
  local copies, waits for them, and re-layouts  6.96 us (14%)
  between operations  0.74 us (1%)
    pallas_call x1, Pallas kernels, local(): pl.pallas_call(functools.partial(brick_kernel, dims, counts), out_shape=(...  24.3 us
    pallas_call x1, Pallas kernels, local(): pl.pallas_call(functools.partial(compose_kernel, counts, views), out_shap...  9.63 us
    pallas_call x1, Pallas kernels, local(): pl.pallas_call(functools.partial(halo_kernel, dims, counts), out_shape=(l...  8.35 us
    unnamed x26, local copies, waits for them, and re-layouts  6.96 us

profile of v1, /device:TPU:0, one launch (start us, length us, event | category | flops | bytes accessed | tf_op | source)
XLA Modules:
  0.0 50.0 jit_solution(10006827260285473906)
XLA Ops:
  0.6 0.0 copy-start
  0.6 0.0 copy-start.9
  0.6 0.0 copy-start.10
  0.7 8.3 %shard_map.68 = (f32[64,128]{1,0:T(8,128)}, f32[64,128]{1,0:T(8,128)}, f32[32,128]{1,0:T(8,128)}, f32[32,128]{1,0:T(8,128)}) custom-call(f32[2048,128]{1,0:T(8,128)} %bitcast.1), custom_call_target="tpu_custom_call" | custom-call | tf_op jit(solution)/shard_map/pallas_call | solution.py:259
  9.0 0.0 copy-start.8
  9.0 0.0 copy-start.7
  9.0 0.0 copy-done
  9.0 0.0 copy-done.9
  9.1 0.0 copy-done.10
  9.1 0.6 %copy-done.8 = s32[4,128]{1,0:T(4,128)S(1)} copy-done((s32[4,128]{1,0:T(4,128)S(1)}, s32[4,128]{1,0:T(4,128)}, u32[]{:S(2)}) %copy-start.8) | copy-done | bytes 2072
  9.7 0.0 copy-done.7
  9.7 0.0 copy-start.3
  9.7 0.8 %copy-done.3 = f32[64,128]{1,0:T(8,128)S(1)} copy-done((f32[64,128]{1,0:T(8,128)S(1)}, f32[64,128]{1,0:T(8,128)}, u32[]{:S(2)}) %copy-start.3) | copy-done | bytes 32792
  10.5 0.0 copy-start.4
  10.5 0.8 %copy-done.4 = f32[64,128]{1,0:T(8,128)S(1)} copy-done((f32[64,128]{1,0:T(8,128)S(1)}, f32[64,128]{1,0:T(8,128)}, u32[]{:S(2)}) %copy-start.4) | copy-done | bytes 32792
  11.2 0.0 copy-start.5
  11.2 0.7 %copy-done.5 = f32[32,128]{1,0:T(8,128)S(1)} copy-done((f32[32,128]{1,0:T(8,128)S(1)}, f32[32,128]{1,0:T(8,128)}, u32[]{:S(2)}) %copy-start.5) | copy-done | bytes 16408
  11.9 0.0 copy-start.6
  11.9 0.7 %copy-done.6 = f32[32,128]{1,0:T(8,128)S(1)} copy-done((f32[32,128]{1,0:T(8,128)S(1)}, f32[32,128]{1,0:T(8,128)}, u32[]{:S(2)}) %copy-start.6) | copy-done | bytes 16408
  12.7 24.3 %shard_map.69 = (f32[8,8,8,128]{3,2,1,0:T(8,128)S(1)}, f32[4,8,8,128]{3,2,1,0:T(8,128)S(1)}) custom-call(f32[2048,128]{1,0:T(8,128)S(1)} %bitcast.2, s32[4,128]{1,0:T(4,128)S(1)} %copy-done.8, s32[2,32]{1,0:T(2,128)S(1)} %copy-done.9, s32[2,64]{1,0:T(2,128)S(1)} %copy-done.10, s32[2,2]{1,0:T(2,128)S(1)} %copy-done.7, f32[64,128]{1,0:T(8,128)S(1)} %copy-done.3, ...), custom_call_target="tpu_custom_call" | custom-call | tf_op jit(solution)/shard_map/pallas_call | solution.py:272
  37.0 0.0 copy-start.1
  37.0 0.7 %copy-done.1 = f32[8,8,8,128]{3,2,1,0:T(8,128)} copy-done((f32[8,8,8,128]{3,2,1,0:T(8,128)}, f32[8,8,8,128]{3,2,1,0:T(8,128)S(1)}, u32[]{:S(2)}) %copy-start.1) | copy-done | bytes 262168
  37.7 0.0 copy-start.2
  37.7 0.6 %copy-done.2 = f32[4,8,8,128]{3,2,1,0:T(8,128)} copy-done((f32[4,8,8,128]{3,2,1,0:T(8,128)}, f32[4,8,8,128]{3,2,1,0:T(8,128)S(1)}, u32[]{:S(2)}) %copy-start.2) | copy-done | bytes 131096
  38.4 9.6 %shard_map.70 = (f32[2,4,8,128]{3,2,1,0:T(8,128)}, f32[2,4,8,128]{3,2,1,0:T(8,128)}) custom-call(s32[2,2]{1,0:T(2,128)} %direction.3, f32[8,8,8,128]{3,2,1,0:T(8,128)} %copy-done.1, f32[4,8,8,128]{3,2,1,0:T(8,128)} %copy-done.2), custom_call_target="tpu_custom_call" | custom-call | tf_op jit(solution)/shard_map/pallas_call | solution.py:286
  48.0 0.0 copy-start.11
  48.0 1.4 %copy.9 = f32[2,4,8,128]{3,2,1,0:T(8,128)} copy(f32[2,4,8,128]{3,2,1,0:T(8,128)} %get-tuple-element.16) | data formatting | bytes 65536
  49.4 0.0 copy-done.11
  49.4 0.6 %copy.10 = f32[2,4,8,128]{3,2,1,0:T(8,128)} copy(f32[2,4,8,128]{3,2,1,0:T(8,128)S(1)} %copy-done.11) | data formatting | bytes 65536
Async XLA Ops:
  0.6 8.4 %copy-start = (f32[32,64,128]{2,1,0:T(8,128)S(1)}, f32[32,64,128]{2,1,0:T(8,128)}, u32[]{:S(2)}) copy-start(f32[32,64,128]{2,1,0:T(8,128)} %param.5) | copy-start | bytes 3145732
  0.6 8.4 %copy-start.9 = (s32[2,32]{1,0:T(2,128)S(1)}, s32[2,32]{1,0:T(2,128)}, u32[]{:S(2)}) copy-start(s32[2,32]{1,0:T(2,128)} %shear_x.1) | copy-start | bytes 772
  0.6 8.4 %copy-start.10 = (s32[2,64]{1,0:T(2,128)S(1)}, s32[2,64]{1,0:T(2,128)}, u32[]{:S(2)}) copy-start(s32[2,64]{1,0:T(2,128)} %shear_y.1) | copy-start | bytes 1540
  9.0 0.7 %copy-start.8 = (s32[4,128]{1,0:T(4,128)S(1)}, s32[4,128]{1,0:T(4,128)}, u32[]{:S(2)}) copy-start(s32[4,128]{1,0:T(4,128)} %table.1) | copy-start | bytes 6148
  9.0 0.7 %copy-start.7 = (s32[2,2]{1,0:T(2,128)S(1)}, s32[2,2]{1,0:T(2,128)}, u32[]{:S(2)}) copy-start(s32[2,2]{1,0:T(2,128)} %direction.3) | copy-start | bytes 52
  9.7 0.8 %copy-start.3 = (f32[64,128]{1,0:T(8,128)S(1)}, f32[64,128]{1,0:T(8,128)}, u32[]{:S(2)}) copy-start(f32[64,128]{1,0:T(8,128)} %get-tuple-element.8.halo_x_low) | copy-start | bytes 98308
  10.5 0.8 %copy-start.4 = (f32[64,128]{1,0:T(8,128)S(1)}, f32[64,128]{1,0:T(8,128)}, u32[]{:S(2)}) copy-start(f32[64,128]{1,0:T(8,128)} %get-tuple-element.9.halo_x_high) | copy-start | bytes 98308
  11.2 0.7 %copy-start.5 = (f32[32,128]{1,0:T(8,128)S(1)}, f32[32,128]{1,0:T(8,128)}, u32[]{:S(2)}) copy-start(f32[32,128]{1,0:T(8,128)} %get-tuple-element.10.halo_y_low) | copy-start | bytes 49156
  11.9 0.7 %copy-start.6 = (f32[32,128]{1,0:T(8,128)S(1)}, f32[32,128]{1,0:T(8,128)}, u32[]{:S(2)}) copy-start(f32[32,128]{1,0:T(8,128)} %get-tuple-element.11.halo_y_high) | copy-start | bytes 49156
  37.0 0.7 %copy-start.1 = (f32[8,8,8,128]{3,2,1,0:T(8,128)}, f32[8,8,8,128]{3,2,1,0:T(8,128)S(1)}, u32[]{:S(2)}) copy-start(f32[8,8,8,128]{3,2,1,0:T(8,128)S(1)} %get-tuple-element.12.parts_x) | copy-start | bytes 786436
  37.7 0.7 %copy-start.2 = (f32[4,8,8,128]{3,2,1,0:T(8,128)}, f32[4,8,8,128]{3,2,1,0:T(8,128)S(1)}, u32[]{:S(2)}) copy-start(f32[4,8,8,128]{3,2,1,0:T(8,128)S(1)} %get-tuple-element.13.parts_y) | copy-start | bytes 393220
  48.0 1.4 %copy-start.11 = (f32[2,4,8,128]{3,2,1,0:T(8,128)S(1)}, f32[2,4,8,128]{3,2,1,0:T(8,128)}, u32[]{:S(2)}) copy-start(f32[2,4,8,128]{3,2,1,0:T(8,128)} %get-tuple-element.17) | copy-start | bytes 98308

commit v2 on v1

--- a/solution.py
+++ b/solution.py
@@ -10,7 +10,7 @@
 
 MESH = pl.DeviceIdType.MESH
 LOG2E = math.log2(math.e)
-UNROLL = 4
+UNROLL = 16
 
 
 def take(row, places):
@@ -119,14 +119,27 @@
 
 def brick_kernel(
     dims, counts,
-    density, table, shear_x, shear_y, direction,
-    halo_x_low, halo_x_high, halo_y_low, halo_y_high,
-    parts_x, parts_y, fields_x, fields_y,
+    density_far, table, shear_x, shear_y, direction,
+    far_x_low, far_x_high, far_y_low, far_y_high,
+    parts_x, parts_y, fields_x, fields_y, density,
+    halo_x_low, halo_x_high, halo_y_low, halo_y_high, loads,
 ):
     depth_x, depth_y, cells_z = dims
     count_x, count_y = counts
     views = shear_x.shape[0]
     knots = table.shape[1]
+
+    fetches = [
+        pltpu.make_async_copy(far, near, loads.at[k])
+        for k, (far, near) in enumerate((
+            (density_far, density),
+            (far_x_low, halo_x_low), (far_x_high, halo_x_high),
+            (far_y_low, halo_y_low), (far_y_high, halo_y_high),
+        ))
+    ]
+    for fetch in fetches:
+        fetch.start()
+    fetches[0].wait()
 
     step_x = 2.0 * LOG2E / (depth_x * count_x)
     step_y = 2.0 * LOG2E / (depth_y * count_y)
@@ -147,8 +160,10 @@
                 fields_y[c, pl.ds(x, depth_y, stride=depth_x), :] = value * step_y
         return 0
 
-    lax.fori_loop(0, depth_x, classify, 0)
-
+    lax.fori_loop(0, depth_x, classify, 0, unroll=2)
+
+    for fetch in fetches[1:]:
+        fetch.wait()
     lanes = lax.broadcasted_iota(jnp.int32, (depth_y, cells_z), 1)
     ranks = lax.broadcasted_iota(jnp.int32, (depth_y, cells_z), 0)
 
@@ -186,7 +201,7 @@
         return 0
 
     shade(0, halo_x_low[...], plane(0), plane(1))
-    lax.fori_loop(1, depth_x - 1, shade_inner, 0)
+    lax.fori_loop(1, depth_x - 1, shade_inner, 0, unroll=2)
     shade(depth_x - 1, plane(depth_x - 2), plane(depth_x - 1), halo_x_high[...])
 
     for fields, shear, family, count, depth, across, parts in (
@@ -217,8 +232,12 @@
             pl.semaphore_signal(
                 barrier, inc=1, device_id={axis: lax.rem(me + step, count)}, device_id_type=MESH
             )
-    got_x[me_x] = parts_x[me_x]
-    got_y[me_y] = parts_y[me_y]
+    own = [
+        pltpu.make_async_copy(parts_x.at[me_x], got_x.at[me_x], recv_x.at[0]),
+        pltpu.make_async_copy(parts_y.at[me_y], got_y.at[me_y], recv_y.at[0]),
+    ]
+    for copy in own:
+        copy.start()
     pl.semaphore_wait(barrier, count_x + count_y - 2)
     groups = []
     for axis, me, count, parts, got, send, recv in (
@@ -236,6 +255,7 @@
     ):
         for copy in group:
             copy.wait_recv()
+        own[family].wait()
         compose(got, direction, family, count, views, image)
     for group in groups:
         for copy in group:
@@ -253,6 +273,7 @@
     cells = depth_x * depth_y
     vmem = pl.BlockSpec(memory_space=pltpu.VMEM)
     smem = pl.BlockSpec(memory_space=pltpu.SMEM)
+    far = pl.BlockSpec(memory_space=pl.ANY)
     density = density.reshape(cells, cells_z)
     layer_x = jax.ShapeDtypeStruct((depth_y, cells_z), f32)
     layer_y = jax.ShapeDtypeStruct((depth_x, cells_z), f32)
@@ -275,11 +296,17 @@
             jax.ShapeDtypeStruct((count_x, views * 4, piece_x, cells_z), f32),
             jax.ShapeDtypeStruct((count_y, views * 4, piece_y, cells_z), f32),
         ),
-        in_specs=[vmem, vmem, smem, smem, smem] + [vmem] * 4,
+        in_specs=[far, vmem, smem, smem, smem] + [far] * 4,
         out_specs=(vmem, vmem),
         scratch_shapes=[
             pltpu.VMEM((4, cells, cells_z), f32),
             pltpu.VMEM((4, cells, cells_z), f32),
+            pltpu.VMEM((cells, cells_z), f32),
+            pltpu.VMEM((depth_y, cells_z), f32),
+            pltpu.VMEM((depth_y, cells_z), f32),
+            pltpu.VMEM((depth_x, cells_z), f32),
+            pltpu.VMEM((depth_x, cells_z), f32),
+            pltpu.SemaphoreType.DMA((5,)),
         ],
         compiler_params=pltpu.CompilerParams(vmem_limit_bytes=40 * 2**20),
     )(density, transfer_table, shear_x, shear_y, direction, *halos)
@@ -289,7 +316,7 @@
             jax.ShapeDtypeStruct((views, 4, piece_x, cells_z), f32),
             jax.ShapeDtypeStruct((views, 4, piece_y, cells_z), f32),
         ),
-        in_specs=[smem, vmem, vmem],
+        in_specs=[smem, far, far],
         out_specs=(vmem, vmem),
         scratch_shapes=[
             pltpu.VMEM((count_x, views * 4, piece_x, cells_z), f32),

time: 50.5 us -> 44.9 us (0.89)
  Pallas kernels: 42.3 us -> 36.7 us
    pallas_call x1, Pallas kernels: 24.3 us -> 18.8 us  [local(): pl.pallas_call(functools.partial(brick_kernel, dims, counts), out_shape=(...]
where the time goes in v2:
time: 44.9 us; the launch traced here: 44.4 us
  Pallas kernels  36.7 us (82%)
  local copies, waits for them, and re-layouts  6.96 us (16%)
  between operations  0.74 us (2%)
    pallas_call x1, Pallas kernels, local(): pl.pallas_call(functools.partial(brick_kernel, dims, counts), out_shape=(...  18.8 us
    pallas_call x1, Pallas kernels, local(): pl.pallas_call(functools.partial(compose_kernel, counts, views), out_shap...  9.53 us
    pallas_call x1, Pallas kernels, local(): pl.pallas_call(functools.partial(halo_kernel, dims, counts), out_shape=(l...  8.35 us
    unnamed x26, local copies, waits for them, and re-layouts  6.96 us

profile of v2, /device:TPU:0, one launch (start us, length us, event | category | flops | bytes accessed | tf_op | source)
XLA Modules:
  0.0 44.4 jit_solution(7936066077961215619)
XLA Ops:
  0.6 0.0 copy-start
  0.6 0.0 copy-start.9
  0.6 0.0 copy-start.10
  0.7 8.3 %shard_map.68 = (f32[64,128]{1,0:T(8,128)}, f32[64,128]{1,0:T(8,128)}, f32[32,128]{1,0:T(8,128)}, f32[32,128]{1,0:T(8,128)}) custom-call(f32[2048,128]{1,0:T(8,128)} %bitcast.1), custom_call_target="tpu_custom_call" | custom-call | tf_op jit(solution)/shard_map/pallas_call | solution.py:280
  9.0 0.0 copy-start.8
  9.0 0.0 copy-start.7
  9.0 0.0 copy-done
  9.0 0.0 copy-done.9
  9.1 0.0 copy-done.10
  9.1 0.6 %copy-done.8 = s32[4,128]{1,0:T(4,128)S(1)} copy-done((s32[4,128]{1,0:T(4,128)S(1)}, s32[4,128]{1,0:T(4,128)}, u32[]{:S(2)}) %copy-start.8) | copy-done | bytes 2072
  9.7 0.0 copy-done.7
  9.7 0.0 copy-start.3
  9.7 0.8 %copy-done.3 = f32[64,128]{1,0:T(8,128)S(1)} copy-done((f32[64,128]{1,0:T(8,128)S(1)}, f32[64,128]{1,0:T(8,128)}, u32[]{:S(2)}) %copy-start.3) | copy-done | bytes 32792
  10.5 0.0 copy-start.4
  10.5 0.8 %copy-done.4 = f32[64,128]{1,0:T(8,128)S(1)} copy-done((f32[64,128]{1,0:T(8,128)S(1)}, f32[64,128]{1,0:T(8,128)}, u32[]{:S(2)}) %copy-start.4) | copy-done | bytes 32792
  11.2 0.0 copy-start.5
  11.2 0.7 %copy-done.5 = f32[32,128]{1,0:T(8,128)S(1)} copy-done((f32[32,128]{1,0:T(8,128)S(1)}, f32[32,128]{1,0:T(8,128)}, u32[]{:S(2)}) %copy-start.5) | copy-done | bytes 16408
  11.9 0.0 copy-start.6
  11.9 0.7 %copy-done.6 = f32[32,128]{1,0:T(8,128)S(1)} copy-done((f32[32,128]{1,0:T(8,128)S(1)}, f32[32,128]{1,0:T(8,128)}, u32[]{:S(2)}) %copy-start.6) | copy-done | bytes 16408
  12.7 18.8 %shard_map.69 = (f32[8,8,8,128]{3,2,1,0:T(8,128)S(1)}, f32[4,8,8,128]{3,2,1,0:T(8,128)S(1)}) custom-call(f32[2048,128]{1,0:T(8,128)S(1)} %bitcast.2, s32[4,128]{1,0:T(4,128)S(1)} %copy-done.8, s32[2,32]{1,0:T(2,128)S(1)} %copy-done.9, s32[2,64]{1,0:T(2,128)S(1)} %copy-done.10, s32[2,2]{1,0:T(2,128)S(1)} %copy-done.7, f32[64,128]{1,0:T(8,128)S(1)} %copy-done.3, ...), custom_call_target="tpu_custom_call" | custom-call | tf_op jit(solution)/shard_map/pallas_call | solution.py:293
  31.5 0.0 copy-start.1
  31.5 0.7 %copy-done.1 = f32[8,8,8,128]{3,2,1,0:T(8,128)} copy-done((f32[8,8,8,128]{3,2,1,0:T(8,128)}, f32[8,8,8,128]{3,2,1,0:T(8,128)S(1)}, u32[]{:S(2)}) %copy-start.1) | copy-done | bytes 262168
  32.2 0.0 copy-start.2
  32.2 0.6 %copy-done.2 = f32[4,8,8,128]{3,2,1,0:T(8,128)} copy-done((f32[4,8,8,128]{3,2,1,0:T(8,128)}, f32[4,8,8,128]{3,2,1,0:T(8,128)S(1)}, u32[]{:S(2)}) %copy-start.2) | copy-done | bytes 131096
  32.8 9.5 %shard_map.70 = (f32[2,4,8,128]{3,2,1,0:T(8,128)}, f32[2,4,8,128]{3,2,1,0:T(8,128)}) custom-call(s32[2,2]{1,0:T(2,128)} %direction.3, f32[8,8,8,128]{3,2,1,0:T(8,128)} %copy-done.1, f32[4,8,8,128]{3,2,1,0:T(8,128)} %copy-done.2), custom_call_target="tpu_custom_call" | custom-call | tf_op jit(solution)/shard_map/pallas_call | solution.py:313
  42.4 0.0 copy-start.11
  42.4 1.4 %copy.9 = f32[2,4,8,128]{3,2,1,0:T(8,128)} copy(f32[2,4,8,128]{3,2,1,0:T(8,128)} %get-tuple-element.16) | data formatting | bytes 65536
  43.8 0.0 copy-done.11
  43.8 0.6 %copy.10 = f32[2,4,8,128]{3,2,1,0:T(8,128)} copy(f32[2,4,8,128]{3,2,1,0:T(8,128)S(1)} %copy-done.11) | data formatting | bytes 65536
Async XLA Ops:
  0.6 8.4 %copy-start = (f32[32,64,128]{2,1,0:T(8,128)S(1)}, f32[32,64,128]{2,1,0:T(8,128)}, u32[]{:S(2)}) copy-start(f32[32,64,128]{2,1,0:T(8,128)} %param.5) | copy-start | bytes 3145732
  0.6 8.4 %copy-start.9 = (s32[2,32]{1,0:T(2,128)S(1)}, s32[2,32]{1,0:T(2,128)}, u32[]{:S(2)}) copy-start(s32[2,32]{1,0:T(2,128)} %shear_x.1) | copy-start | bytes 772
  0.6 8.4 %copy-start.10 = (s32[2,64]{1,0:T(2,128)S(1)}, s32[2,64]{1,0:T(2,128)}, u32[]{:S(2)}) copy-start(s32[2,64]{1,0:T(2,128)} %shear_y.1) | copy-start | bytes 1540
  9.0 0.7 %copy-start.8 = (s32[4,128]{1,0:T(4,128)S(1)}, s32[4,128]{1,0:T(4,128)}, u32[]{:S(2)}) copy-start(s32[4,128]{1,0:T(4,128)} %table.1) | copy-start | bytes 6148
  9.0 0.7 %copy-start.7 = (s32[2,2]{1,0:T(2,128)S(1)}, s32[2,2]{1,0:T(2,128)}, u32[]{:S(2)}) copy-start(s32[2,2]{1,0:T(2,128)} %direction.3) | copy-start | bytes 52
  9.7 0.8 %copy-start.3 = (f32[64,128]{1,0:T(8,128)S(1)}, f32[64,128]{1,0:T(8,128)}, u32[]{:S(2)}) copy-start(f32[64,128]{1,0:T(8,128)} %get-tuple-element.8.far_x_low) | copy-start | bytes 98308
  10.5 0.8 %copy-start.4 = (f32[64,128]{1,0:T(8,128)S(1)}, f32[64,128]{1,0:T(8,128)}, u32[]{:S(2)}) copy-start(f32[64,128]{1,0:T(8,128)} %get-tuple-element.9.far_x_high) | copy-start | bytes 98308
  11.2 0.7 %copy-start.5 = (f32[32,128]{1,0:T(8,128)S(1)}, f32[32,128]{1,0:T(8,128)}, u32[]{:S(2)}) copy-start(f32[32,128]{1,0:T(8,128)} %get-tuple-element.10.far_y_low) | copy-start | bytes 49156
  11.9 0.7 %copy-start.6 = (f32[32,128]{1,0:T(8,128)S(1)}, f32[32,128]{1,0:T(8,128)}, u32[]{:S(2)}) copy-start(f32[32,128]{1,0:T(8,128)} %get-tuple-element.11.far_y_high) | copy-start | bytes 49156
  31.5 0.7 %copy-start.1 = (f32[8,8,8,128]{3,2,1,0:T(8,128)}, f32[8,8,8,128]{3,2,1,0:T(8,128)S(1)}, u32[]{:S(2)}) copy-start(f32[8,8,8,128]{3,2,1,0:T(8,128)S(1)} %get-tuple-element.12.parts_x) | copy-start | bytes 786436
  32.2 0.7 %copy-start.2 = (f32[4,8,8,128]{3,2,1,0:T(8,128)}, f32[4,8,8,128]{3,2,1,0:T(8,128)S(1)}, u32[]{:S(2)}) copy-start(f32[4,8,8,128]{3,2,1,0:T(8,128)S(1)} %get-tuple-element.13.parts_y) | copy-start | bytes 393220
  42.4 1.4 %copy-start.11 = (f32[2,4,8,128]{3,2,1,0:T(8,128)S(1)}, f32[2,4,8,128]{3,2,1,0:T(8,128)}, u32[]{:S(2)}) copy-start(f32[2,4,8,128]{3,2,1,0:T(8,128)} %get-tuple-element.17) | copy-start | bytes 98308

commit v3 on v1

v3 whole, which is shorter than its diff:
```python
import functools
import math

import jax
import jax.numpy as jnp
from jax import lax
from jax.experimental import pallas as pl
from jax.experimental.pallas import tpu as pltpu
from jax.sharding import PartitionSpec as P

MESH = pl.DeviceIdType.MESH
LOG2E = math.log2(math.e)
UNROLL = 16


def take(row, places):
    return jnp.take_along_axis(
        jnp.broadcast_to(row, places.shape), places, axis=1, mode="promise_in_bounds"
    )


def exchange_copy(parts, received, send_sem, recv_sem, axis, me, count, step):
    target = lax.rem(me + step, count)
    return pltpu.make_async_remote_copy(
        src_ref=parts.at[target],
        dst_ref=received.at[me],
        send_sem=send_sem.at[step],
        recv_sem=recv_sem.at[step],
        device_id={axis: target},
        device_id_type=MESH,
    )


def march(fields, shear_ref, direction_ref, family, view, depth, pitch, begin, rows, cells_z):
    lanes = lax.broadcasted_iota(jnp.int32, (rows, cells_z), 1)
    upwards = jnp.full((rows, cells_z), direction_ref[family, view], jnp.int32) == 0

    def step(i, carried):
        behind, colours = carried
        shift = shear_ref[view, i]
        amount = jnp.where(shift < 0, shift + cells_z, shift)
        inside = (lanes >= shift) & (lanes < cells_z + shift)
        at = pl.ds(pl.multiple_of(i * pitch + begin, 8), rows)
        sheared = [pltpu.roll(fields[c, at, :], amount, 1) for c in range(4)]
        optical = jnp.where(inside, sheared[3], 0.0)
        through = jnp.exp2(-jnp.where(upwards, behind, optical))
        kept = jnp.where(upwards, 1.0, through)
        added = jnp.where(inside, jnp.where(upwards, through, 1.0), 0.0)
        colours = tuple(total * kept + added * sheared[c] for c, total in enumerate(colours))
        return behind + optical, colours

    zero = jnp.zeros((rows, cells_z), jnp.float32)
    return lax.fori_loop(0, depth, step, (zero, (zero, zero, zero)), unroll=UNROLL)


def compose(received, direction_ref, family, count, views, out_ref):
    for view in range(views):
        turned = direction_ref[family, view].astype(jnp.float32)
        depths = [received[i, view * 4 + 3] for i in range(count)]
        lower, upper = [jnp.zeros_like(depths[0])], [jnp.zeros_like(depths[0])]
        for i in range(count):
            lower.append(lower[-1] + depths[i])
            upper.append(upper[-1] + depths[count - 1 - i])
        through = [
            jnp.exp2(-(lower[i] * (1.0 - turned) + upper[count - 1 - i] * turned))
            for i in range(count)
        ]
        for c in range(3):
            total = through[0] * received[0, view * 4 + c]
            for i in range(1, count):
                total += through[i] * received[i, view * 4 + c]
            out_ref[view, c] = total
        out_ref[view, 3] = 1.0 - jnp.exp2(-lower[-1])


def classify_kernel(rows, step, density, table, classed):
    knots = table.shape[1]
    levels = table[...].astype(jnp.float32) * (1.0 / 255.0)
    rises = pltpu.roll(levels, knots - 1, 1) - levels

    def classify(x, _):
        at = pl.ds(pl.multiple_of(x * rows, 8), rows)
        scaled = density[at, :] * (knots - 1.0)
        places = jnp.minimum(scaled.astype(jnp.int32), knots - 1)
        rest = scaled - places.astype(jnp.float32)
        for c in range(4):
            value = take(levels[c:c + 1], places) + rest * take(rises[c:c + 1], places)
            classed[c, at, :] = value if c < 3 else value * step
        return 0

    lax.fori_loop(0, density.shape[0] // rows, classify, 0, unroll=2)


def kernel(
    dims, counts,
    density, classed, shear_x, shear_y, direction,
    image_x, image_y,
    fields_x, fields_y, face_low, face_high,
    halo_x_low, halo_x_high, halo_y_low, halo_y_high,
    parts_x, got_x, parts_y, got_y,
    halo_send, halo_recv, send_x, recv_x, send_y, recv_y, load_sem,
):
    depth_x, depth_y, cells_z = dims
    count_x, count_y = counts
    views = shear_x.shape[0]
    me_x, me_y = lax.axis_index("gx"), lax.axis_index("gy")

    loading = pltpu.make_async_copy(classed, fields_x, load_sem)
    loading.start()
    barrier = pltpu.get_barrier_semaphore()
    for axis, me, count in (("gx", me_x, count_x), ("gy", me_y, count_y)):
        for step in range(1, count):
            pl.semaphore_signal(
                barrier, inc=1, device_id={axis: lax.rem(me + step, count)}, device_id_type=MESH
            )
    face_low[...] = density[pl.ds(0, depth_x, stride=depth_y), :]
    face_high[...] = density[pl.ds(depth_y - 1, depth_x, stride=depth_y), :]
    pl.semaphore_wait(barrier, count_x + count_y - 2)

    last = (depth_x - 1) * depth_y
    halos = []
    for k, (axis, me, count, delta, src, dst) in enumerate((
        ("gx", me_x, count_x, 1, density.at[pl.ds(last, depth_y), :], halo_x_low),
        ("gx", me_x, count_x, -1, density.at[pl.ds(0, depth_y), :], halo_x_high),
        ("gy", me_y, count_y, 1, face_high, halo_y_low),
        ("gy", me_y, count_y, -1, face_low, halo_y_high),
    )):
        copy = pltpu.make_async_remote_copy(
            src_ref=src, dst_ref=dst, send_sem=halo_send.at[k], recv_sem=halo_recv.at[k],
            device_id={axis: lax.rem(me + delta + count, count)}, device_id_type=MESH,
        )
        sends = me < count - 1 if delta == 1 else me > 0
        receives = me > 0 if delta == 1 else me < count - 1
        halos.append((copy, sends, receives, dst))
        pl.when(sends)(copy.start)

    step_x = 2.0 * LOG2E / (depth_x * count_x)
    step_y = 2.0 * LOG2E / (depth_y * count_y)

    loading.wait()

    def turn(x, _):
        at = pl.ds(pl.multiple_of(x * depth_y, 8), depth_y)
        fields_y[3, pl.ds(x, depth_y, stride=depth_x), :] = fields_x[3, at, :] * (step_y / step_x)
        return 0

    lax.fori_loop(0, depth_x, turn, 0, unroll=2)

    for copy, sends, receives, dst in halos:
        pl.when(receives)(copy.wait_recv)

        @pl.when(jnp.logical_not(receives))
        def _():
            dst[...] = jnp.zeros_like(dst)

    lanes = lax.broadcasted_iota(jnp.int32, (depth_y, cells_z), 1)
    ranks = lax.broadcasted_iota(jnp.int32, (depth_y, cells_z), 0)

    def shade(x, before, here, after):
        low = halo_y_low[pl.ds(x, 1), :]
        high = halo_y_high[pl.ds(x, 1), :]
        rise_x = after - before
        rise_y = jnp.where(ranks == depth_y - 1, high, pltpu.roll(here, depth_y - 1, 0)) - jnp.where(
            ranks == 0, low, pltpu.roll(here, 1, 0)
        )
        rise_z = jnp.where(lanes == cells_z - 1, 0.0, pltpu.roll(here, cells_z - 1, 1)) - jnp.where(
            lanes == 0, 0.0, pltpu.roll(here, 1, 1)
        )
        facing = jnp.abs(rise_x + 2.0 * (rise_y + rise_z)) * (0.7 / 3.0)
        steep = rise_x * rise_x + rise_y * rise_y + rise_z * rise_z + 0.04
        shaded = 0.3 + facing * lax.rsqrt(steep)
        at = pl.ds(pl.multiple_of(x * depth_y, 8), depth_y)
        turned_at = pl.ds(x, depth_y, stride=depth_x)
        optical = fields_x[3, at, :]
        gain_x = shaded * (1.0 - jnp.exp2(-optical))
        if step_x == step_y:
            gain_y = gain_x
        else:
            gain_y = shaded * (1.0 - jnp.exp2(-(optical * (step_y / step_x))))
        for c in range(3):
            colour = fields_x[c, at, :]
            fields_x[c, at, :] = colour * gain_x
            fields_y[c, turned_at, :] = colour * gain_y

    def plane(x):
        return density[pl.ds(pl.multiple_of(x * depth_y, 8), depth_y), :]

    def shade_inner(x, _):
        shade(x, plane(x - 1), plane(x), plane(x + 1))
        return 0

    shade(0, halo_x_low[...], plane(0), plane(1))
    lax.fori_loop(1, depth_x - 1, shade_inner, 0, unroll=2)
    shade(depth_x - 1, plane(depth_x - 2), plane(depth_x - 1), halo_x_high[...])

    copies = []
    for fields, shear, family, axis, me, count, depth, across, parts, got, send, recv in (
        (fields_x, shear_x, 0, "gx", me_x, count_x, depth_x, depth_y, parts_x, got_x, send_x, recv_x),
        (fields_y, shear_y, 1, "gy", me_y, count_y, depth_y, depth_x, parts_y, got_y, send_y, recv_y),
    ):
        piece = across // count
        rows = math.gcd(across, 32)
        for view in range(views):
            for begin in range(0, across, rows):
                behind, colours = march(
                    fields, shear, direction, family, view, depth, across, begin, rows, cells_z
                )
                for c, result in enumerate(colours + (behind,)):
                    for r in range(0, rows, piece):
                        parts[(begin + r) // piece, view * 4 + c] = result[r:r + piece]
        group = [
            exchange_copy(parts, got, send, recv, axis, me, count, step) for step in range(1, count)
        ]
        for copy in group:
            copy.start()
        got[me] = parts[me]
        copies.append(group)

    for copy in copies[0]:
        copy.wait_recv()
    compose(got_x, direction, 0, count_x, views, image_x)
    for copy in copies[1]:
        copy.wait_recv()
    compose(got_y, direction, 1, count_y, views, image_y)

    for copy, sends, receives, dst in halos:
        pl.when(sends)(copy.wait_send)
    for group in copies:
        for copy in group:
            copy.wait_send()


def local(density, transfer_table, shear_x, shear_y, direction):
    count_x, count_y = lax.axis_size("gx"), lax.axis_size("gy")
    depth_x, depth_y, cells_z = density.shape
    views = shear_x.shape[0]
    f32 = jnp.float32
    piece_x, piece_y = depth_y // count_x, depth_x // count_y
    cells = depth_x * depth_y
    vmem = pl.BlockSpec(memory_space=pltpu.VMEM)
    smem = pl.BlockSpec(memory_space=pltpu.SMEM)
    density = density.reshape(cells, cells_z)
    layers = math.gcd(depth_x, 8)
    classed = pl.pallas_call(
        functools.partial(classify_kernel, depth_y, 2.0 * LOG2E / (depth_x * count_x)),
        grid=(depth_x // layers,),
        out_shape=jax.ShapeDtypeStruct((4, cells, cells_z), f32),
        in_specs=[
            pl.BlockSpec((layers * depth_y, cells_z), lambda i: (i, 0)),
            pl.BlockSpec(transfer_table.shape, lambda i: (0, 0)),
        ],
        out_specs=pl.BlockSpec((4, layers * depth_y, cells_z), lambda i: (0, i, 0)),
    )(density, transfer_table)
    return tuple(pl.pallas_call(
        functools.partial(kernel, (depth_x, depth_y, cells_z), (count_x, count_y)),
        out_shape=(
            jax.ShapeDtypeStruct((views, 4, piece_x, cells_z), f32),
            jax.ShapeDtypeStruct((views, 4, piece_y, cells_z), f32),
        ),
        in_specs=[vmem, pl.BlockSpec(memory_space=pltpu.HBM), smem, smem, smem],
        out_specs=(vmem, vmem),
        scratch_shapes=[
            pltpu.VMEM((4, cells, cells_z), f32),
            pltpu.VMEM((4, cells, cells_z), f32),
            pltpu.VMEM((depth_x, cells_z), f32),
            pltpu.VMEM((depth_x, cells_z), f32),
            pltpu.VMEM((depth_y, cells_z), f32),
            pltpu.VMEM((depth_y, cells_z), f32),
            pltpu.VMEM((depth_x, cells_z), f32),
            pltpu.VMEM((depth_x, cells_z), f32),
            pltpu.VMEM((count_x, views * 4, piece_x, cells_z), f32),
            pltpu.VMEM((count_x, views * 4, piece_x, cells_z), f32),
            pltpu.VMEM((count_y, views * 4, piece_y, cells_z), f32),
            pltpu.VMEM((count_y, views * 4, piece_y, cells_z), f32),
            pltpu.SemaphoreType.DMA((4,)),
            pltpu.SemaphoreType.DMA((4,)),
            pltpu.SemaphoreType.DMA((count_x,)),
            pltpu.SemaphoreType.DMA((count_x,)),
            pltpu.SemaphoreType.DMA((count_y,)),
            pltpu.SemaphoreType.DMA((count_y,)),
            pltpu.SemaphoreType.DMA,
        ],
        compiler_params=pltpu.CompilerParams(
            collective_id=0, has_side_effects=True, vmem_limit_bytes=40 * 2**20
        ),
    )(density, classed, shear_x, shear_y, direction))


def solution(mesh):
    placed = (P("gx", "gy", None), P(), P(None, "gx"), P(None, "gy"), P())
    return jax.shard_map(
        local,
        mesh=mesh,
        in_specs=placed,
        out_specs=(P(None, None, ("gy", "gx"), None), P(None, None, ("gx", "gy"), None)),
        check_vma=False,
    )
```

time: 50.5 us -> 37.8 us (0.75)
  Pallas kernels: 42.3 us -> 33.5 us
  local copies, waits for them, and re-layouts: 6.96 us -> 3.43 us
    pallas_call x3 -> x2, Pallas kernels: 42.3 us -> 33.5 us  [the longest x1 24.2 us: local(): pl.pallas_call(functools.partial(kernel, (depth_x, depth_y, cells_z), (co...]
    unnamed x26 -> x12, local copies, waits for them, and re-layouts: 6.96 us -> 3.43 us
where the time goes in v3:
time: 37.8 us; the launch traced here: 37.6 us
  Pallas kernels  33.5 us (89%)
  local copies, waits for them, and re-layouts  3.43 us (9%)
  between operations  0.69 us (2%)
    pallas_call x1, Pallas kernels, local(): pl.pallas_call(functools.partial(kernel, (depth_x, depth_y, cells_z), (co...  24.2 us
    pallas_call x1, Pallas kernels, local(): pl.pallas_call(functools.partial(classify_kernel, depth_y, 2.0 * LOG2E /...  9.29 us
    unnamed x12, local copies, waits for them, and re-layouts  3.43 us

profile of v3, /device:TPU:0, one launch (start us, length us, event | category | flops | bytes accessed | tf_op | source)
XLA Modules:
  0.0 37.6 jit_solution(2061074243607467005)
XLA Ops:
  0.6 0.0 copy-start.4
  0.6 0.0 copy-start.3
  0.7 0.0 copy-start.2
  0.7 0.0 copy-start.1
  0.7 9.3 %shard_map.68.classed = f32[4,2048,128]{2,1,0:T(8,128)} custom-call(f32[2048,128]{1,0:T(8,128)} %bitcast.1, s32[4,128]{1,0:T(4,128)} %table.1), custom_call_target="tpu_custom_call" | custom-call | tf_op jit(solution)/shard_map/pallas_call | solution.py:244
  10.0 0.0 copy-done.4
  10.0 0.0 copy-done.3
  10.0 0.0 copy-done.2
  10.0 0.0 copy-done.1
  10.0 0.0 copy-start
  10.0 2.2 %copy-done = f32[4,2048,128]{2,1,0:T(8,128)S(1)} copy-done((f32[4,2048,128]{2,1,0:T(8,128)S(1)}, f32[4,2048,128]{2,1,0:T(8,128)}, u32[]{:S(2)}) %copy-start) | copy-done | bytes 4194328
  12.2 24.2 %shard_map.69 = (f32[2,4,8,128]{3,2,1,0:T(8,128)S(1)}, f32[2,4,8,128]{3,2,1,0:T(8,128)S(1)}) custom-call(f32[2048,128]{1,0:T(8,128)S(1)} %bitcast.2, f32[4,2048,128]{2,1,0:T(8,128)S(1)} %copy-done, s32[2,32]{1,0:T(2,128)S(1)} %copy-done.2, s32[2,64]{1,0:T(2,128)S(1)} %copy-done.3, s32[2,2]{1,0:T(2,128)S(1)} %copy-done.4), custom_call_target="tpu_custom_call" | custom-call | tf_op jit(solution)/shard_map/pallas_call | solution.py:254
  36.4 0.6 %copy.9 = f32[2,4,8,128]{3,2,1,0:T(8,128)} copy(f32[2,4,8,128]{3,2,1,0:T(8,128)S(1)} %get-tuple-element.4) | data formatting | bytes 65536
  37.0 0.6 %copy.10 = f32[2,4,8,128]{3,2,1,0:T(8,128)} copy(f32[2,4,8,128]{3,2,1,0:T(8,128)S(1)} %get-tuple-element.5) | data formatting | bytes 65536
Async XLA Ops:
  0.6 9.3 %copy-start.4 = (s32[2,2]{1,0:T(2,128)S(1)}, s32[2,2]{1,0:T(2,128)}, u32[]{:S(2)}) copy-start(s32[2,2]{1,0:T(2,128)} %direction.1) | copy-start | bytes 52
  0.6 9.3 %copy-start.3 = (s32[2,64]{1,0:T(2,128)S(1)}, s32[2,64]{1,0:T(2,128)}, u32[]{:S(2)}) copy-start(s32[2,64]{1,0:T(2,128)} %shear_y.1) | copy-start | bytes 1540
  0.7 9.3 %copy-start.2 = (s32[2,32]{1,0:T(2,128)S(1)}, s32[2,32]{1,0:T(2,128)}, u32[]{:S(2)}) copy-start(s32[2,32]{1,0:T(2,128)} %shear_x.1) | copy-start | bytes 772
  0.7 9.3 %copy-start.1 = (f32[32,64,128]{2,1,0:T(8,128)S(1)}, f32[32,64,128]{2,1,0:T(8,128)}, u32[]{:S(2)}) copy-start(f32[32,64,128]{2,1,0:T(8,128)} %param.5) | copy-start | bytes 3145732
  10.0 2.2 %copy-start = (f32[4,2048,128]{2,1,0:T(8,128)S(1)}, f32[4,2048,128]{2,1,0:T(8,128)}, u32[]{:S(2)}) copy-start(f32[4,2048,128]{2,1,0:T(8,128)} %shard_map.68.classed) | copy-start | bytes 12582916

commit v4 on v3

--- a/solution.py
+++ b/solution.py
@@ -73,46 +73,53 @@
         out_ref[view, 3] = 1.0 - jnp.exp2(-lower[-1])
 
 
-def classify_kernel(rows, step, density, table, classed):
+def classify(density, table, scales):
     knots = table.shape[1]
-    levels = table[...].astype(jnp.float32) * (1.0 / 255.0)
-    rises = pltpu.roll(levels, knots - 1, 1) - levels
-
-    def classify(x, _):
-        at = pl.ds(pl.multiple_of(x * rows, 8), rows)
-        scaled = density[at, :] * (knots - 1.0)
-        places = jnp.minimum(scaled.astype(jnp.int32), knots - 1)
-        rest = scaled - places.astype(jnp.float32)
-        for c in range(4):
-            value = take(levels[c:c + 1], places) + rest * take(rises[c:c + 1], places)
-            classed[c, at, :] = value if c < 3 else value * step
-        return 0
-
-    lax.fori_loop(0, density.shape[0] // rows, classify, 0, unroll=2)
+    packed = table[3:4] * 2**24 + table[2:3] * 2**16 + table[1:2] * 2**8 + table[0:1]
+    scaled = density * (knots - 1.0)
+    places = jnp.minimum(scaled.astype(jnp.int32), knots - 1)
+    rest = scaled - places.astype(jnp.float32)
+    low, high = take(packed, places), take(pltpu.roll(packed, knots - 1, 1), places)
+    values = []
+    for c in range(4):
+        lower = (lax.shift_right_logical(low, 8 * c) & 255).astype(jnp.float32)
+        upper = (lax.shift_right_logical(high, 8 * c) & 255).astype(jnp.float32)
+        values.append((lower + rest * (upper - lower)) * scales[c])
+    return values
 
 
 def kernel(
     dims, counts,
-    density, classed, shear_x, shear_y, direction,
+    density_far, table, shear_x, shear_y, direction,
     image_x, image_y,
     fields_x, fields_y, face_low, face_high,
     halo_x_low, halo_x_high, halo_y_low, halo_y_high,
     parts_x, got_x, parts_y, got_y,
-    halo_send, halo_recv, send_x, recv_x, send_y, recv_y, load_sem,
+    halo_send, halo_recv, send_x, recv_x, send_y, recv_y, density, load_sem,
 ):
     depth_x, depth_y, cells_z = dims
     count_x, count_y = counts
     views = shear_x.shape[0]
     me_x, me_y = lax.axis_index("gx"), lax.axis_index("gy")
 
-    loading = pltpu.make_async_copy(classed, fields_x, load_sem)
-    loading.start()
+    quarter = density.shape[0] // 4
+    loading = [
+        pltpu.make_async_copy(
+            density_far.at[pl.ds(k * quarter, quarter), :],
+            density.at[pl.ds(k * quarter, quarter), :], load_sem.at[k],
+        )
+        for k in range(4)
+    ]
+    for copy in loading:
+        copy.start()
     barrier = pltpu.get_barrier_semaphore()
     for axis, me, count in (("gx", me_x, count_x), ("gy", me_y, count_y)):
         for step in range(1, count):
             pl.semaphore_signal(
                 barrier, inc=1, device_id={axis: lax.rem(me + step, count)}, device_id_type=MESH
             )
+    for copy in loading:
+        copy.wait()
     face_low[...] = density[pl.ds(0, depth_x, stride=depth_y), :]
     face_high[...] = density[pl.ds(depth_y - 1, depth_x, stride=depth_y), :]
     pl.semaphore_wait(barrier, count_x + count_y - 2)
@@ -137,14 +144,18 @@
     step_x = 2.0 * LOG2E / (depth_x * count_x)
     step_y = 2.0 * LOG2E / (depth_y * count_y)
 
-    loading.wait()
-
-    def turn(x, _):
+    levels = table[...]
+    scales = (1.0 / 255.0, 1.0 / 255.0, 1.0 / 255.0, step_x / 255.0)
+
+    def look_up(x, _):
         at = pl.ds(pl.multiple_of(x * depth_y, 8), depth_y)
-        fields_y[3, pl.ds(x, depth_y, stride=depth_x), :] = fields_x[3, at, :] * (step_y / step_x)
+        values = classify(density[at, :], levels, scales)
+        for c in range(4):
+            fields_x[c, at, :] = values[c]
+        fields_y[3, pl.ds(x, depth_y, stride=depth_x), :] = values[3] * (step_y / step_x)
         return 0
 
-    lax.fori_loop(0, depth_x, turn, 0, unroll=2)
+    lax.fori_loop(0, depth_x, look_up, 0, unroll=2)
 
     for copy, sends, receives, dst in halos:
         pl.when(receives)(copy.wait_recv)
@@ -240,24 +251,13 @@
     vmem = pl.BlockSpec(memory_space=pltpu.VMEM)
     smem = pl.BlockSpec(memory_space=pltpu.SMEM)
     density = density.reshape(cells, cells_z)
-    layers = math.gcd(depth_x, 8)
-    classed = pl.pallas_call(
-        functools.partial(classify_kernel, depth_y, 2.0 * LOG2E / (depth_x * count_x)),
-        grid=(depth_x // layers,),
-        out_shape=jax.ShapeDtypeStruct((4, cells, cells_z), f32),
-        in_specs=[
-            pl.BlockSpec((layers * depth_y, cells_z), lambda i: (i, 0)),
-            pl.BlockSpec(transfer_table.shape, lambda i: (0, 0)),
-        ],
-        out_specs=pl.BlockSpec((4, layers * depth_y, cells_z), lambda i: (0, i, 0)),
-    )(density, transfer_table)
     return tuple(pl.pallas_call(
         functools.partial(kernel, (depth_x, depth_y, cells_z), (count_x, count_y)),
         out_shape=(
             jax.ShapeDtypeStruct((views, 4, piece_x, cells_z), f32),
             jax.ShapeDtypeStruct((views, 4, piece_y, cells_z), f32),
         ),
-        in_specs=[vmem, pl.BlockSpec(memory_space=pltpu.HBM), smem, smem, smem],
+        in_specs=[pl.BlockSpec(memory_space=pltpu.HBM), vmem, smem, smem, smem],
         out_specs=(vmem, vmem),
         scratch_shapes=[
             pltpu.VMEM((4, cells, cells_z), f32),
@@ -278,12 +278,13 @@
             pltpu.SemaphoreType.DMA((count_x,)),
             pltpu.SemaphoreType.DMA((count_y,)),
             pltpu.SemaphoreType.DMA((count_y,)),
-            pltpu.SemaphoreType.DMA,
+            pltpu.VMEM((cells, cells_z), f32),
+            pltpu.SemaphoreType.DMA((4,)),
         ],
         compiler_params=pltpu.CompilerParams(
             collective_id=0, has_side_effects=True, vmem_limit_bytes=40 * 2**20
         ),
-    )(density, classed, shear_x, shear_y, direction))
+    )(density, transfer_table, shear_x, shear_y, direction))
 
 
 def solution(mesh):

time: 37.8 us -> 31.4 us (0.83)
  Pallas kernels: 33.5 us -> 25.4 us
  local copies, waits for them, and re-layouts: 3.43 us -> 5.17 us
    pallas_call x1 -> x0, Pallas kernels: 9.29 us -> none  [local(): pl.pallas_call(functools.partial(classify_kernel, depth_y, 2.0 * LOG2E /...]
    unnamed x12, local copies, waits for them, and re-layouts: 3.43 us -> 5.17 us
    pallas_call x1, Pallas kernels: 24.2 us -> 25.4 us  [local(): pl.pallas_call(functools.partial(kernel, (depth_x, depth_y, cells_z), (co...]
where the time goes in v4:
time: 31.4 us; the launch traced here: 31.2 us
  Pallas kernels  25.4 us (81%)
  local copies, waits for them, and re-layouts  5.17 us (16%)
  between operations  0.65 us (2%)
    pallas_call x1, Pallas kernels, local(): pl.pallas_call(functools.partial(kernel, (depth_x, depth_y, cells_z), (co...  25.4 us
    unnamed x12, local copies, waits for them, and re-layouts  5.17 us

profile of v4, /device:TPU:0, one launch (start us, length us, event | category | flops | bytes accessed | tf_op | source)
XLA Modules:
  0.0 31.2 jit_solution(2475191917141777469)
XLA Ops:
  0.6 0.0 copy-start.2
  0.6 0.7 %copy-done.2 = s32[2,32]{1,0:T(2,128)S(1)} copy-done((s32[2,32]{1,0:T(2,128)S(1)}, s32[2,32]{1,0:T(2,128)}, u32[]{:S(2)}) %copy-start.2) | copy-done | bytes 280
  1.3 0.0 copy-start
  1.3 1.2 %copy-done = f32[32,64,128]{2,1,0:T(8,128)S(1)} copy-done((f32[32,64,128]{2,1,0:T(8,128)S(1)}, f32[32,64,128]{2,1,0:T(8,128)}, u32[]{:S(2)}) %copy-start) | copy-done | bytes 1048600
  2.5 0.0 copy-start.1
  2.5 0.7 %copy-done.1 = s32[4,128]{1,0:T(4,128)S(1)} copy-done((s32[4,128]{1,0:T(4,128)S(1)}, s32[4,128]{1,0:T(4,128)}, u32[]{:S(2)}) %copy-start.1) | copy-done | bytes 2072
  3.2 0.0 copy-start.3
  3.2 0.7 %copy-done.3 = s32[2,64]{1,0:T(2,128)S(1)} copy-done((s32[2,64]{1,0:T(2,128)S(1)}, s32[2,64]{1,0:T(2,128)}, u32[]{:S(2)}) %copy-start.3) | copy-done | bytes 536
  3.9 0.0 copy-start.4
  3.9 0.7 %copy-done.4 = s32[2,2]{1,0:T(2,128)S(1)} copy-done((s32[2,2]{1,0:T(2,128)S(1)}, s32[2,2]{1,0:T(2,128)}, u32[]{:S(2)}) %copy-start.4) | copy-done | bytes 40
  4.6 25.4 %shard_map.68 = (f32[2,4,8,128]{3,2,1,0:T(8,128)S(1)}, f32[2,4,8,128]{3,2,1,0:T(8,128)S(1)}) custom-call(f32[2048,128]{1,0:T(8,128)S(1)} %bitcast.1, s32[4,128]{1,0:T(4,128)S(1)} %copy-done.1, s32[2,32]{1,0:T(2,128)S(1)} %copy-done.2, s32[2,64]{1,0:T(2,128)S(1)} %copy-done.3, s32[2,2]{1,0:T(2,128)S(1)} %copy-done.4), custom_call_target="tpu_custom_call" | custom-call | tf_op jit(solution)/shard_map/pallas_call | solution.py:254
  30.0 0.6 %copy.9 = f32[2,4,8,128]{3,2,1,0:T(8,128)} copy(f32[2,4,8,128]{3,2,1,0:T(8,128)S(1)} %get-tuple-element.4) | data formatting | bytes 65536
  30.6 0.6 %copy.10 = f32[2,4,8,128]{3,2,1,0:T(8,128)} copy(f32[2,4,8,128]{3,2,1,0:T(8,128)S(1)} %get-tuple-element.5) | data formatting | bytes 65536
Async XLA Ops:
  0.6 0.7 %copy-start.2 = (s32[2,32]{1,0:T(2,128)S(1)}, s32[2,32]{1,0:T(2,128)}, u32[]{:S(2)}) copy-start(s32[2,32]{1,0:T(2,128)} %shear_x.1) | copy-start | bytes 772
  1.3 1.2 %copy-start = (f32[32,64,128]{2,1,0:T(8,128)S(1)}, f32[32,64,128]{2,1,0:T(8,128)}, u32[]{:S(2)}) copy-start(f32[32,64,128]{2,1,0:T(8,128)} %param.5) | copy-start | bytes 3145732
  2.5 0.7 %copy-start.1 = (s32[4,128]{1,0:T(4,128)S(1)}, s32[4,128]{1,0:T(4,128)}, u32[]{:S(2)}) copy-start(s32[4,128]{1,0:T(4,128)} %table.1) | copy-start | bytes 6148
  3.2 0.7 %copy-start.3 = (s32[2,64]{1,0:T(2,128)S(1)}, s32[2,64]{1,0:T(2,128)}, u32[]{:S(2)}) copy-start(s32[2,64]{1,0:T(2,128)} %shear_y.1) | copy-start | bytes 1540
  3.9 0.7 %copy-start.4 = (s32[2,2]{1,0:T(2,128)S(1)}, s32[2,2]{1,0:T(2,128)}, u32[]{:S(2)}) copy-start(s32[2,2]{1,0:T(2,128)} %direction.1) | copy-start | bytes 52

commit v5 on v4

--- a/solution.py
+++ b/solution.py
@@ -90,12 +90,12 @@
 
 def kernel(
     dims, counts,
-    density_far, table, shear_x, shear_y, direction,
+    density_far, table_far, shear_x_far, shear_y_far, direction_far,
     image_x, image_y,
     fields_x, fields_y, face_low, face_high,
     halo_x_low, halo_x_high, halo_y_low, halo_y_high,
     parts_x, got_x, parts_y, got_y,
-    halo_send, halo_recv, send_x, recv_x, send_y, recv_y, density, load_sem,
+    halo_send, halo_recv, send_x, recv_x, send_y, recv_y, density, table, shear_x, shear_y, direction, load_sem, small_sem,
 ):
     depth_x, depth_y, cells_z = dims
     count_x, count_y = counts
@@ -110,7 +110,14 @@
         )
         for k in range(4)
     ]
-    for copy in loading:
+    small = [
+        pltpu.make_async_copy(source, target, small_sem.at[k])
+        for k, (source, target) in enumerate((
+            (table_far, table), (shear_x_far, shear_x),
+            (shear_y_far, shear_y), (direction_far, direction),
+        ))
+    ]
+    for copy in loading + small:
         copy.start()
     barrier = pltpu.get_barrier_semaphore()
     for axis, me, count in (("gx", me_x, count_x), ("gy", me_y, count_y)):
@@ -118,7 +125,7 @@
             pl.semaphore_signal(
                 barrier, inc=1, device_id={axis: lax.rem(me + step, count)}, device_id_type=MESH
             )
-    for copy in loading:
+    for copy in loading + small:
         copy.wait()
     face_low[...] = density[pl.ds(0, depth_x, stride=depth_y), :]
     face_high[...] = density[pl.ds(depth_y - 1, depth_x, stride=depth_y), :]
@@ -249,7 +256,6 @@
     piece_x, piece_y = depth_y // count_x, depth_x // count_y
     cells = depth_x * depth_y
     vmem = pl.BlockSpec(memory_space=pltpu.VMEM)
-    smem = pl.BlockSpec(memory_space=pltpu.SMEM)
     density = density.reshape(cells, cells_z)
     return tuple(pl.pallas_call(
         functools.partial(kernel, (depth_x, depth_y, cells_z), (count_x, count_y)),
@@ -257,7 +263,7 @@
             jax.ShapeDtypeStruct((views, 4, piece_x, cells_z), f32),
             jax.ShapeDtypeStruct((views, 4, piece_y, cells_z), f32),
         ),
-        in_specs=[pl.BlockSpec(memory_space=pltpu.HBM), vmem, smem, smem, smem],
+        in_specs=[pl.BlockSpec(memory_space=pltpu.HBM)] * 5,
         out_specs=(vmem, vmem),
         scratch_shapes=[
             pltpu.VMEM((4, cells, cells_z), f32),
@@ -279,10 +285,15 @@
             pltpu.SemaphoreType.DMA((count_y,)),
             pltpu.SemaphoreType.DMA((count_y,)),
             pltpu.VMEM((cells, cells_z), f32),
+            pltpu.VMEM(transfer_table.shape, jnp.int32),
+            pltpu.SMEM(shear_x.shape, jnp.int32),
+            pltpu.SMEM(shear_y.shape, jnp.int32),
+            pltpu.SMEM(direction.shape, jnp.int32),
+            pltpu.SemaphoreType.DMA((4,)),
             pltpu.SemaphoreType.DMA((4,)),
         ],
         compiler_params=pltpu.CompilerParams(
-            collective_id=0, has_side_effects=True, vmem_limit_bytes=40 * 2**20
+            collective_id=0, has_side_effects=True, vmem_limit_bytes=64 * 2**20
         ),
     )(density, transfer_table, shear_x, shear_y, direction))
 

time: 31.4 us -> 28.3 us (0.901)
  local copies, waits for them, and re-layouts: 5.17 us -> 2 us
    unnamed x12 -> x4, local copies, waits for them, and re-layouts: 5.17 us -> 2 us
where the time goes in v5:
time: 28.3 us; the launch traced here: 28.1 us
  Pallas kernels  25.4 us (90%)
  local copies, waits for them, and re-layouts  2 us (7%)
  between operations  0.65 us (2%)
    pallas_call x1, Pallas kernels, local(): pl.pallas_call(functools.partial(kernel, (depth_x, depth_y, cells_z), (co...  25.4 us
    unnamed x4, local copies, waits for them, and re-layouts  2 us

profile of v5, /device:TPU:0, one launch (start us, length us, event | category | flops | bytes accessed | tf_op | source)
XLA Modules:
  0.0 28.1 jit_solution(2421543182362553149)
XLA Ops:
  0.6 25.4 %shard_map.68 = (f32[2,4,8,128]{3,2,1,0:T(8,128)}, f32[2,4,8,128]{3,2,1,0:T(8,128)}) custom-call(f32[2048,128]{1,0:T(8,128)} %bitcast.1, s32[4,128]{1,0:T(4,128)} %table_far.1, s32[2,32]{1,0:T(2,128)} %shear_x_far.1, s32[2,64]{1,0:T(2,128)} %shear_y_far.1, s32[2,2]{1,0:T(2,128)} %direction_far.1), custom_call_target="tpu_custom_call" | custom-call | tf_op jit(solution)/shard_map/pallas_call | solution.py:260
  26.1 0.0 copy-start
  26.1 1.4 %copy.9 = f32[2,4,8,128]{3,2,1,0:T(8,128)} copy(f32[2,4,8,128]{3,2,1,0:T(8,128)} %get-tuple-element.4) | data formatting | bytes 65536
  27.4 0.0 copy-done
  27.4 0.6 %copy.10 = f32[2,4,8,128]{3,2,1,0:T(8,128)} copy(f32[2,4,8,128]{3,2,1,0:T(8,128)S(1)} %copy-done) | data formatting | bytes 65536
Async XLA Ops:
  26.1 1.4 %copy-start = (f32[2,4,8,128]{3,2,1,0:T(8,128)S(1)}, f32[2,4,8,128]{3,2,1,0:T(8,128)}, u32[]{:S(2)}) copy-start(f32[2,4,8,128]{3,2,1,0:T(8,128)} %get-tuple-element.5) | copy-start | bytes 98308

commit v6 on v5

--- a/solution.py
+++ b/solution.py
@@ -19,13 +19,13 @@
     )
 
 
-def exchange_copy(parts, received, send_sem, recv_sem, axis, me, count, step):
+def exchange_copy(parts, received, send_sem, recv_sem, axis, me, count, step, view):
     target = lax.rem(me + step, count)
     return pltpu.make_async_remote_copy(
-        src_ref=parts.at[target],
-        dst_ref=received.at[me],
-        send_sem=send_sem.at[step],
-        recv_sem=recv_sem.at[step],
+        src_ref=parts.at[target, pl.ds(view * 4, 4)],
+        dst_ref=received.at[me, pl.ds(view * 4, 4)],
+        send_sem=send_sem.at[view, step],
+        recv_sem=recv_sem.at[view, step],
         device_id={axis: target},
         device_id_type=MESH,
     )
@@ -33,7 +33,9 @@
 
 def march(fields, shear_ref, direction_ref, family, view, depth, pitch, begin, rows, cells_z):
     lanes = lax.broadcasted_iota(jnp.int32, (rows, cells_z), 1)
-    upwards = jnp.full((rows, cells_z), direction_ref[family, view], jnp.int32) == 0
+    turned = jnp.full((rows, cells_z), direction_ref[family, view], jnp.int32)
+    upwards = turned == 0
+    sign = (2 * turned - 1).astype(jnp.float32)
 
     def step(i, carried):
         behind, colours = carried
@@ -42,15 +44,16 @@
         inside = (lanes >= shift) & (lanes < cells_z + shift)
         at = pl.ds(pl.multiple_of(i * pitch + begin, 8), rows)
         sheared = [pltpu.roll(fields[c, at, :], amount, 1) for c in range(4)]
-        optical = jnp.where(inside, sheared[3], 0.0)
-        through = jnp.exp2(-jnp.where(upwards, behind, optical))
-        kept = jnp.where(upwards, 1.0, through)
-        added = jnp.where(inside, jnp.where(upwards, through, 1.0), 0.0)
-        colours = tuple(total * kept + added * sheared[c] for c, total in enumerate(colours))
-        return behind + optical, colours
+        after = behind + jnp.where(inside, sheared[3] * sign, 0.0)
+        through = jnp.where(inside, jnp.exp2(jnp.where(upwards, behind, after)), 0.0)
+        colours = tuple(total + through * sheared[c] for c, total in enumerate(colours))
+        return after, colours
 
     zero = jnp.zeros((rows, cells_z), jnp.float32)
-    return lax.fori_loop(0, depth, step, (zero, (zero, zero, zero)), unroll=UNROLL)
+    signed, colours = lax.fori_loop(0, depth, step, (zero, (zero, zero, zero)), unroll=UNROLL)
+    summed = signed * sign
+    rest = jnp.where(upwards, 1.0, jnp.exp2(-summed))
+    return summed, tuple(total * rest for total in colours)
 
 
 def compose(received, direction_ref, family, count, views, out_ref):
@@ -218,6 +221,7 @@
     ):
         piece = across // count
         rows = math.gcd(across, 32)
+        group = []
         for view in range(views):
             for begin in range(0, across, rows):
                 behind, colours = march(
@@ -226,11 +230,13 @@
                 for c, result in enumerate(colours + (behind,)):
                     for r in range(0, rows, piece):
                         parts[(begin + r) // piece, view * 4 + c] = result[r:r + piece]
-        group = [
-            exchange_copy(parts, got, send, recv, axis, me, count, step) for step in range(1, count)
-        ]
-        for copy in group:
-            copy.start()
+            sent = [
+                exchange_copy(parts, got, send, recv, axis, me, count, step, view)
+                for step in range(1, count)
+            ]
+            for copy in sent:
+                copy.start()
+            group += sent
         got[me] = parts[me]
         copies.append(group)
 
@@ -280,10 +286,10 @@
             pltpu.VMEM((count_y, views * 4, piece_y, cells_z), f32),
             pltpu.SemaphoreType.DMA((4,)),
             pltpu.SemaphoreType.DMA((4,)),
-            pltpu.SemaphoreType.DMA((count_x,)),
-            pltpu.SemaphoreType.DMA((count_x,)),
-            pltpu.SemaphoreType.DMA((count_y,)),
-            pltpu.SemaphoreType.DMA((count_y,)),
+            pltpu.SemaphoreType.DMA((views, count_x)),
+            pltpu.SemaphoreType.DMA((views, count_x)),
+            pltpu.SemaphoreType.DMA((views, count_y)),
+            pltpu.SemaphoreType.DMA((views, count_y)),
             pltpu.VMEM((cells, cells_z), f32),
             pltpu.VMEM(transfer_table.shape, jnp.int32),
             pltpu.SMEM(shear_x.shape, jnp.int32),

time: 28.3 us -> 28.1 us (level)
  no operation moved by 1% of the time
where the time goes in v6:
time: 28.1 us; the launch traced here: 27.9 us
  Pallas kernels  25.3 us (90%)
  local copies, waits for them, and re-layouts  2 us (7%)
  between operations  0.65 us (2%)
    pallas_call x1, Pallas kernels, local(): pl.pallas_call(functools.partial(kernel, (depth_x, depth_y, cells_z), (co...  25.3 us
    unnamed x4, local copies, waits for them, and re-layouts  2 us

profile of v6, /device:TPU:0, one launch (start us, length us, event | category | flops | bytes accessed | tf_op | source)
XLA Modules:
  0.0 27.9 jit_solution(13389384567853154158)
XLA Ops:
  0.6 25.3 %shard_map.68 = (f32[2,4,8,128]{3,2,1,0:T(8,128)}, f32[2,4,8,128]{3,2,1,0:T(8,128)}) custom-call(f32[2048,128]{1,0:T(8,128)} %bitcast.1, s32[4,128]{1,0:T(4,128)} %table_far.1, s32[2,32]{1,0:T(2,128)} %shear_x_far.1, s32[2,64]{1,0:T(2,128)} %shear_y_far.1, s32[2,2]{1,0:T(2,128)} %direction_far.1), custom_call_target="tpu_custom_call" | custom-call | tf_op jit(solution)/shard_map/pallas_call | solution.py:266
  25.9 0.0 copy-start
  25.9 1.4 %copy.9 = f32[2,4,8,128]{3,2,1,0:T(8,128)} copy(f32[2,4,8,128]{3,2,1,0:T(8,128)} %get-tuple-element.4) | data formatting | bytes 65536
  27.3 0.0 copy-done
  27.3 0.6 %copy.10 = f32[2,4,8,128]{3,2,1,0:T(8,128)} copy(f32[2,4,8,128]{3,2,1,0:T(8,128)S(1)} %copy-done) | data formatting | bytes 65536
Async XLA Ops:
  25.9 1.4 %copy-start = (f32[2,4,8,128]{3,2,1,0:T(8,128)S(1)}, f32[2,4,8,128]{3,2,1,0:T(8,128)}, u32[]{:S(2)}) copy-start(f32[2,4,8,128]{3,2,1,0:T(8,128)} %get-tuple-element.5) | copy-start | bytes 98308
